TPU v7x, 128 devices: a whole 4x4x4 slice. The times are simulated.
128 devices in a mesh: seq: 16 (over y, z), head: 8 (over x, core).
Axes of the slice: x: 4, y: 4, z: 4, core: 2. Of those that a mesh axis runs over, the one named last changes fastest.
Arguments:
- modulation: bfloat16 [16384, 4608], P(('seq', 'head')), may hold values from -3 to 3
- latents: bfloat16 [16384, 16], P(('seq', 'head')), may hold values from -6 to 6
- noise: bfloat16 [16384, 64], P(('seq', 'head')), may hold values from -6 to 6
- times: bfloat16 [16384, 4], P(('seq', 'head')), may hold values from 0.019897461 to 0.9765625
- image_rows: int32 [128], P(('seq', 'head')), may hold values from 1 to 128, 8192 in all
- in_weight: bfloat16 [16, 1536], replicated, may hold values from -1.5 to 1.5
- fc1_weight: bfloat16 [1536, 1536], replicated, may hold values from -0.15625 to 0.15625
- fc2_weight: bfloat16 [1536, 1536], replicated, may hold values from -0.15625 to 0.15625
- out_weight: bfloat16 [16, 1536], replicated, may hold values from -0.15625 to 0.15625
Outputs:
- mod_grad: float32 [16384, 4608], P(('seq', 'head'))
- fc1_grad: float32 [1536, 1536], P(('seq', 'head'))
- fc2_grad: float32 [1536, 1536], P(('seq', 'head'))
- in_grad: float32 [16, 1536], P(None, ('seq', 'head'))
- out_grad: float32 [16, 1536], P(None, ('seq', 'head'))
Inputs may be any that keep to these rules, and one draw needn't show every extreme that they name: `image_rows`: the counts sum to exactly 8192; a device's image tokens are its first rows.
All inputs are finite; a program needn't handle non-finite values.
Results may differ from a plain program's by a relative error of at most 0.005.
The roundings to bfloat16 on the way count: a program that leaves them out, or rounds other values in their place, can miss the bound.
Values may be sent and summed in bfloat16 or wider, within the bound.
A program may use at most 128 MiB of HBM per device.

v0:
```python
import jax
import jax.numpy as jnp
from jax import lax
from jax.sharding import PartitionSpec as P

norm_eps = 1e-06


def layer_norm(stream):
    center = stream - jnp.mean(stream, axis=-1, keepdims=True)
    rstd_val = lax.rsqrt(jnp.mean(center * center, axis=-1, keepdims=True) + norm_eps)
    return (center * rstd_val, rstd_val)


def norm_backward(grad_in, normed, rstd_val):
    return rstd_val * (
        grad_in
        - jnp.mean(grad_in, axis=-1, keepdims=True)
        - normed * jnp.mean(grad_in * normed, axis=-1, keepdims=True)
    )


def contract_rows(left_rows, right_rows):
    return lax.dot_general(
        left_rows, right_rows, (((0,), (0,)), ((), ())), preferred_element_type=jnp.float32
    )


def head_pass(
    modulation, latents, noise, times, live_mask, in_weight, fc1_weight, fc2_weight, out_weight
):
    token_count = modulation.shape[0]
    model_width = in_weight.shape[1]
    channel_count = in_weight.shape[0]
    draw_count = times.shape[1]
    mod_values = modulation.astype(jnp.float32)
    shift_part = mod_values[:, :model_width]
    scale_plus = 1.0 + mod_values[:, model_width : 2 * model_width]
    gate_part = mod_values[:, 2 * model_width :]
    noise_draw = (
        noise.astype(jnp.float32).reshape(token_count, draw_count, channel_count).transpose(1, 0, 2)
    )
    angles = 0.5 * jnp.pi * jnp.transpose(times.astype(jnp.float32))[:, :, None]
    noisy_in = (
        jnp.cos(angles) * latents.astype(jnp.float32)[None] + jnp.sin(angles) * noise_draw
    ).astype(jnp.bfloat16)
    noisy_flat = noisy_in.reshape(draw_count * token_count, channel_count)
    stream_in = jnp.dot(noisy_flat, in_weight, preferred_element_type=jnp.float32).reshape(
        draw_count, token_count, model_width
    )
    normed_in, rstd_in = layer_norm(stream_in)
    block_in = (normed_in * scale_plus + shift_part).astype(jnp.bfloat16).reshape(-1, model_width)
    hidden_pre = jnp.dot(block_in, fc1_weight, preferred_element_type=jnp.float32)
    sigmoid_hid = jax.nn.sigmoid(hidden_pre)
    hidden_act = (hidden_pre * sigmoid_hid).astype(jnp.bfloat16)
    branch_out = jnp.dot(hidden_act, fc2_weight, preferred_element_type=jnp.float32).reshape(
        draw_count, token_count, model_width
    )
    stream_out = stream_in + gate_part * branch_out
    normed_out, rstd_out = layer_norm(stream_out)
    final_in = normed_out.astype(jnp.bfloat16).reshape(-1, model_width)
    predicted = jnp.dot(final_in, out_weight.T, preferred_element_type=jnp.float32).reshape(
        draw_count, token_count, channel_count
    )
    pred_grad = (
        (2.0 * (predicted - noise_draw) * live_mask[None, :, None])
        .astype(jnp.bfloat16)
        .reshape(-1, channel_count)
    )
    final_grad = jnp.dot(pred_grad, out_weight, preferred_element_type=jnp.float32).reshape(
        draw_count, token_count, model_width
    )
    stream_grad = norm_backward(final_grad, normed_out, rstd_out)
    branch_grad = (stream_grad * gate_part).astype(jnp.bfloat16).reshape(-1, model_width)
    act_grad = jnp.dot(branch_grad, fc2_weight.T, preferred_element_type=jnp.float32)
    pre_grad = (act_grad * sigmoid_hid * (1.0 + hidden_pre * (1.0 - sigmoid_hid))).astype(
        jnp.bfloat16
    )
    block_grad = jnp.dot(pre_grad, fc1_weight.T, preferred_element_type=jnp.float32).reshape(
        draw_count, token_count, model_width
    )
    input_grad = stream_grad + norm_backward(block_grad * scale_plus, normed_in, rstd_in)
    input_bf = input_grad.astype(jnp.bfloat16).reshape(-1, model_width)
    mod_grad = jnp.concatenate(
        [
            jnp.sum(block_grad, axis=0),
            jnp.sum(block_grad * normed_in, axis=0),
            jnp.sum(stream_grad * branch_out, axis=0),
        ],
        axis=-1,
    )
    return (
        mod_grad,
        (block_in, pre_grad, hidden_act, branch_grad, noisy_flat, input_bf, pred_grad, final_in),
    )


def body(
    modulation, latents, noise, times, image_rows, in_weight, fc1_weight, fc2_weight, out_weight
):
    rows_dev = modulation.shape[0]
    model_width = in_weight.shape[1]
    seq_count = lax.axis_size("seq")
    head_count = lax.axis_size("head")
    dev_count = seq_count * head_count
    factor = (rows_dev * dev_count // 2) ** (-0.5)
    pair_rows = rows_dev // dev_count
    share_rows = rows_dev // 2
    counts = lax.all_gather(image_rows, ("seq", "head"), axis=0, tiled=True)
    offsets = jnp.cumsum(counts) - counts
    my_index = lax.axis_index(("seq", "head"))
    my_offset = offsets[my_index]

    def spread_rows(rows_in):
        return jnp.roll(
            rows_in.reshape((pair_rows, dev_count) + rows_in.shape[1:]), my_offset, axis=1
        )

    outgoing = (
        spread_rows(modulation),
        spread_rows(latents),
        spread_rows(noise),
        spread_rows(times),
    )
    arrived = (
        lax.all_to_all(outgoing[0], ("seq", "head"), split_axis=1, concat_axis=1, tiled=True),
        lax.all_to_all(outgoing[1], ("seq", "head"), split_axis=1, concat_axis=1, tiled=True),
        lax.all_to_all(outgoing[2], ("seq", "head"), split_axis=1, concat_axis=1, tiled=True),
        lax.all_to_all(outgoing[3], ("seq", "head"), split_axis=1, concat_axis=1, tiled=True),
    )
    arrived = tuple(
        (member.reshape((pair_rows * dev_count,) + member.shape[2:]) for member in arrived)
    )
    global_pos = my_index + dev_count * jnp.arange(share_rows, dtype=jnp.int32)
    source_dev = jnp.sum((offsets[None, :] <= global_pos[:, None]).astype(jnp.int32), axis=1) - 1
    within = global_pos - offsets[source_dev]
    slot_index = within // dev_count * dev_count + source_dev
    compact = tuple((jnp.take(member, slot_index, axis=0) for member in arrived))
    live_mask = jnp.ones((share_rows,), jnp.float32)
    compact_grad, pieces = head_pass(
        compact[0],
        compact[1],
        compact[2],
        compact[3],
        live_mask,
        in_weight,
        fc1_weight,
        fc2_weight,
        out_weight,
    )
    entry_ids = jnp.arange(pair_rows * dev_count, dtype=jnp.int32)
    entry_dev = entry_ids % dev_count
    row_in_src = entry_ids // dev_count * dev_count + (my_index - offsets[entry_dev]) % dev_count
    valid_rows = row_in_src < counts[entry_dev]
    back_slot = jnp.clip(
        (offsets[entry_dev] + row_in_src - my_index) // dev_count, 0, share_rows - 1
    )
    returning = jnp.where(valid_rows[:, None], jnp.take(compact_grad, back_slot, axis=0), 0.0)
    returning = returning.reshape(pair_rows, dev_count, -1)
    came_back = lax.all_to_all(returning, ("seq", "head"), split_axis=1, concat_axis=1, tiled=True)
    mod_grad = jnp.roll(came_back, -my_offset, axis=1).reshape(rows_dev, -1)
    block_in, pre_grad, hidden_act, branch_grad, noisy_flat, input_bf, pred_grad, final_in = pieces
    first_part = contract_rows(block_in, pre_grad)
    second_part = contract_rows(hidden_act, branch_grad)
    joined = lax.psum_scatter(
        jnp.concatenate([first_part, second_part], axis=1),
        ("seq", "head"),
        scatter_dimension=0,
        tiled=True,
    )
    fc1_grad = joined[:, :model_width]
    fc2_grad = joined[:, model_width:]
    edge_grads = (
        lax.psum_scatter(
            contract_rows(noisy_flat, input_bf), ("seq", "head"), scatter_dimension=1, tiled=True
        ),
        lax.psum_scatter(
            contract_rows(pred_grad, final_in), ("seq", "head"), scatter_dimension=1, tiled=True
        ),
    )
    return (
        mod_grad,
        fc1_grad * factor,
        fc2_grad * factor,
        edge_grads[0] * factor,
        edge_grads[1] * factor,
    )


def solution(mesh):
    in_specs = (
        P(("seq", "head"), None),
        P(("seq", "head"), None),
        P(("seq", "head"), None),
        P(("seq", "head"), None),
        P(("seq", "head")),
        P(),
        P(),
        P(),
        P(),
    )
    out_specs = (
        P(("seq", "head"), None),
        P(("seq", "head"), None),
        P(("seq", "head"), None),
        P(None, ("seq", "head")),
        P(None, ("seq", "head")),
    )
    return jax.shard_map(body, mesh=mesh, in_specs=in_specs, out_specs=out_specs, check_vma=False)
```

profile of v0, /device:TPU:1, one launch (start us, length us, event | category | flops | bytes accessed | tf_op | source)
XLA Modules:
  0.0 469.5 jit_solution(13915234414624208557)
XLA Ops:
  8.0 68.6 %all-reduce = s32[128]{0:T(128)S(1)} all-reduce(s32[128]{0:T(128)S(1)} %dynamic-update-slice), channel_id=1, replica_groups=mesh['seq'=16,'head'=8] {'seq','head'}, use_global_device_ids=true, to_apply=%add | all-reduce | flops 128 | bytes 1024
  81.1 4.8 %all-to-all-start = ((bf16[1,128,4]{2,0,1:T(2,128)(2,1)}), bf16[1,128,4]{2,0,1:T(2,128)(2,1)S(1)}, u32[]{:S(2)}, u32[]{:S(2)}) async-start(bf16[1,128,4]{2,0,1:T(2,128)(2,1)} %copy.108), calls=%async_computation | async-start | bytes 131072 | tf_op jit(solution)/shard_map/all_to_all | solution.py:129
  86.9 3.1 fusion.6
  90.9 4.4 all-to-all-done
  95.3 5.3 %all-to-all-start.1 = ((bf16[1,128,16]{2,0,1:T(2,128)(2,1)}), bf16[1,128,16]{2,0,1:T(2,128)(2,1)S(1)}, u32[]{:S(2)}, u32[]{:S(2)}) async-start(bf16[1,128,16]{2,0,1:T(2,128)(2,1)} %copy.109), calls=%async_computation.1 | async-start | bytes 131072 | tf_op jit(solution)/shard_map/all_to_all | solution.py:127
  101.5 8.6 %all-to-all-done.1 = bf16[1,128,16]{2,0,1:T(2,128)(2,1)S(1)} async-done(((bf16[1,128,16]{2,0,1:T(2,128)(2,1)}), bf16[1,128,16]{2,0,1:T(2,128)(2,1)S(1)}, u32[]{:S(2)}, u32[]{:S(2)}) %all-to-all-start.1) | async-done | bytes 4128 | tf_op jit(solution)/shard_map/all_to_all | solution.py:127
  110.1 5.2 %all-to-all-start.2 = ((bf16[1,128,64]{2,0,1:T(2,128)(2,1)}), bf16[1,128,64]{2,0,1:T(2,128)(2,1)S(1)}, u32[]{:S(2)}, u32[]{:S(2)}) async-start(bf16[1,128,64]{2,0,1:T(2,128)(2,1)} %copy.90), calls=%async_computation.2 | async-start | bytes 131072 | tf_op jit(solution)/shard_map/all_to_all | solution.py:128
  115.3 3.1 copy.119
  118.9 9.1 %reduce.2 = bf16[128,4608]{1,0:T(8,128)(2,1)} reduce(bf16[128,1,4608]{2,1,0:T(2,128)(2,1)S(1)} %bitcast.118, bf16[]{:T(256)} %broadcast.722), dimensions={1}, to_apply=%bitcast.113.reduce_sub_computation | reduce | bytes 2359298
  128.0 2.2 reshape.592
  131.2 9.8 %all-to-all-start.3 = ((bf16[128,2,2304]{2,1,0:T(2,128)(2,1)}), bf16[128,2,2304]{2,1,0:T(2,128)(2,1)S(1)}, u32[]{:S(2)}, u32[]{:S(2)}) async-start(bf16[128,2,2304]{2,1,0:T(2,128)(2,1)} %reshape.592), calls=%async_computation.3 | async-start | bytes 2359296 | tf_op jit(solution)/shard_map/all_to_all | solution.py:126
  143.4 18.4 %all-to-all-done.3 = bf16[128,2,2304]{2,1,0:T(2,128)(2,1)S(1)} async-done(((bf16[128,2,2304]{2,1,0:T(2,128)(2,1)}), bf16[128,2,2304]{2,1,0:T(2,128)(2,1)S(1)}, u32[]{:S(2)}, u32[]{:S(2)}) %all-to-all-start.3) | async-done | bytes 1179680 | tf_op jit(solution)/shard_map/all_to_all | solution.py:126
  161.7 3.6 reshape.593
  165.3 1.8 copy.116
  169.0 4.6 fusion.43
  173.7 2.6 multiply_add_fusion
  181.3 4.3 fusion.1
  185.6 5.2 %fusion.36 = f32[1536,1536]{0,1:T(8,128)} fusion(bf16[256,1536]{1,0:T(8,128)(2,1)S(1)} %bitcast.128, f32[256,1536]{1,0:T(8,128)S(1)} %copy-done.7), kind=kOutput, calls=%fused_computation.147 | convolution fusion | flops 1209925632 | bytes 11796480 | tf_op jit(solution)/shard_map/dot_general | solution.py:24
  190.8 1.5 fusion.4
  192.3 5.1 %fusion.44 = f32[1536,1536]{0,1:T(8,128)} fusion(bf16[256,1536]{1,0:T(8,128)(2,1)S(1)} %bitcast.126, bf16[256,1536]{1,0:T(8,128)(2,1)S(1)} %fusion.1), kind=kOutput, calls=%fused_computation.155 | convolution fusion | flops 1207959552 | bytes 11010048 | tf_op jit(solution)/shard_map/dot_general | solution.py:24
  198.9 3.7 convolution_bitcast_fusion.1
  202.6 12.6 %pad_maximum_fusion = f32[1536,3072]{0,1:T(8,128)} fusion(f32[1536,1536]{0,1:T(8,128)} %fusion.36, f32[1536,1536]{0,1:T(8,128)} %fusion.44), kind=kLoop, calls=%fused_computation.8 | loop fusion | flops 4718592 | bytes 37748736 | tf_op jit(solution)/shard_map/concatenate | solution.py:166
  215.2 1.4 gather_fusion
  218.1 2.7 gather_fusion.7
  220.8 2.1 fusion.3
  222.9 3.8 copy.95
  226.7 4.3 all-to-all-start.4
  231.7 38.2 %all-to-all-done.4 = f32[1,128,4608]{2,0,1:T(1,128)S(1)} async-done(((f32[1,128,4608]{2,0,1:T(1,128)}), f32[1,128,4608]{2,0,1:T(1,128)S(1)}, u32[]{:S(2)}, u32[]{:S(2)}) %all-to-all-start.4) | async-done | bytes 2359328 | tf_op jit(solution)/shard_map/all_to_all | solution.py:160
  269.9 9.6 %fusion.2 = f32[1,128,4608]{2,0,1:T(1,128)S(1)} fusion(s32[]{:T(128)S(6)} %select_n.256, f32[1,128,4608]{2,0,1:T(1,128)S(1)} %all-to-all-done.4), kind=kLoop, calls=%fused_computation.14 | loop fusion | flops 589824 | bytes 4718596 | tf_op jit(solution)/shard_map/jit(_roll_dynamic)/concatenate | solution.py:161
  279.5 1.6 copy.115
  281.0 174.5 %all-reduce.7.cloned.1.call-done = (f32[1536,3072]{0,1:T(8,128)}, f32[16,1536]{1,0:T(8,128)}, f32[16,1536]{1,0:T(8,128)}) async-done(((f32[1536,3072]{0,1:T(8,128)}, f32[16,1536]{1,0:T(8,128)}, f32[16,1536]{1,0:T(8,128)}), (f32[1536,3072]{0,1:T(8,128)}, f32[16,1536]{1,0:T(8,128)}, f32[16,1536]{1,0:T(8,128)})) %all-reduce.7.cloned.1.call-update) | async-done | bytes 19070992
  455.5 2.4 dynamic-slice_multiply_fusion
  (118 shorter events, 23.4 us)
Async XLA Ops:
  7.2 169.7 %copy-start = (bf16[16,1536]{1,0:T(8,128)(2,1)S(1)}, bf16[16,1536]{1,0:T(8,128)(2,1)}, u32[]{:S(2)}) copy-start(bf16[16,1536]{1,0:T(8,128)(2,1)} %param.17) | copy-start | bytes 147460
  77.0 13.1 %copy-start.18 = (bf16[128,16]{0,1:T(8,128)(2,1)S(1)}, bf16[128,16]{0,1:T(8,128)(2,1)}, u32[]{:S(2)}) copy-start(bf16[128,16]{0,1:T(8,128)(2,1)} %param.10) | copy-start | bytes 12292
  81.1 14.2 %all-to-all-start = ((bf16[1,128,4]{2,0,1:T(2,128)(2,1)}), bf16[1,128,4]{2,0,1:T(2,128)(2,1)S(1)}, u32[]{:S(2)}, u32[]{:S(2)}) async-start(bf16[1,128,4]{2,0,1:T(2,128)(2,1)} %copy.108), calls=%async_computation | async-start | bytes 131072 | tf_op jit(solution)/shard_map/all_to_all | solution.py:129
  85.9 14.8 %copy-start.17 = (bf16[128,64]{0,1:T(8,128)(2,1)S(1)}, bf16[128,64]{0,1:T(8,128)(2,1)}, u32[]{:S(2)}) copy-start(bf16[128,64]{0,1:T(8,128)(2,1)} %param.11) | copy-start | bytes 49156
  95.3 14.8 %all-to-all-start.1 = ((bf16[1,128,16]{2,0,1:T(2,128)(2,1)}), bf16[1,128,16]{2,0,1:T(2,128)(2,1)S(1)}, u32[]{:S(2)}, u32[]{:S(2)}) async-start(bf16[1,128,16]{2,0,1:T(2,128)(2,1)} %copy.109), calls=%async_computation.1 | async-start | bytes 131072 | tf_op jit(solution)/shard_map/all_to_all | solution.py:127
  110.1 21.1 %all-to-all-start.2 = ((bf16[1,128,64]{2,0,1:T(2,128)(2,1)}), bf16[1,128,64]{2,0,1:T(2,128)(2,1)S(1)}, u32[]{:S(2)}, u32[]{:S(2)}) async-start(bf16[1,128,64]{2,0,1:T(2,128)(2,1)} %copy.90), calls=%async_computation.2 | async-start | bytes 131072 | tf_op jit(solution)/shard_map/all_to_all | solution.py:128
  130.3 12.3 %copy-start.16 = (bf16[16,1536]{1,0:T(8,128)(2,1)S(1)}, bf16[16,1536]{1,0:T(8,128)(2,1)}, u32[]{:S(2)}) copy-start(bf16[16,1536]{1,0:T(8,128)(2,1)} %param.14) | copy-start | bytes 147460
  131.2 30.5 %all-to-all-start.3 = ((bf16[128,2,2304]{2,1,0:T(2,128)(2,1)}), bf16[128,2,2304]{2,1,0:T(2,128)(2,1)S(1)}, u32[]{:S(2)}, u32[]{:S(2)}) async-start(bf16[128,2,2304]{2,1,0:T(2,128)(2,1)} %reshape.592), calls=%async_computation.3 | async-start | bytes 2359296 | tf_op jit(solution)/shard_map/all_to_all | solution.py:126
  141.0 314.5 %all-reduce.7.cloned.1.call-start = ((), (), s32[]{:S(2)}) async-start(), calls=%async_computation.5 | async-start | bytes 38141952
  168.3 0.7 copy-start.4
  168.3 5.4 %copy-start.11 = (f32[64,1536]{1,0:T(8,128)}, f32[64,1536]{1,0:T(8,128)S(1)}, u32[]{:S(2)}) copy-start(f32[64,1536]{1,0:T(8,128)S(1)} %get-tuple-element.49) | copy-start | bytes 1179652
  168.3 5.4 %slice-start.2 = ((s8[4718592]{0:T(1024)(128)(4,1)}), s8[4194304]{0:T(1024)(128)(4,1)S(1)}, s32[]{:S(2)}) async-start(s8[4718592]{0:T(1024)(128)(4,1)} %bitcast.123), calls=%async_computation.8 | async-start | bytes 8388608
  169.0 4.7 copy-start.9
  169.0 4.7 slice-start.3
  173.7 2.7 copy-start.6
  178.4 1.4 copy-start.8
  178.4 1.5 copy-start.12
  179.0 2.3 copy-start.2
  179.9 1.4 copy-start.7
  179.9 10.9 %slice-start = ((s8[4718592]{0:T(1024)(128)(4,1)}), s8[4194304]{0:T(1024)(128)(4,1)S(1)}, s32[]{:S(2)}) async-start(s8[4718592]{0:T(1024)(128)(4,1)} %bitcast.121), calls=%async_computation.6 | async-start | bytes 8388608
  181.3 9.5 %slice-start.1 = ((s8[4718592]{0:T(1024)(128)(4,1)}), s8[524288]{0:T(1024)(128)(4,1)S(1)}, s32[]{:S(2)}) async-start(s8[4718592]{0:T(1024)(128)(4,1)} %bitcast.121), calls=%async_computation.7 | async-start | bytes 1048576
  185.6 5.3 %copy-start.5 = (f32[64,1536]{1,0:T(8,128)S(1)}, f32[64,1536]{1,0:T(8,128)}, u32[]{:S(2)}) copy-start(f32[64,1536]{1,0:T(8,128)} %copy-done.4) | copy-start | bytes 1179652
  190.8 1.5 copy-start.10
  192.3 5.1 %copy-start.3 = (f32[256,1536]{1,0:T(8,128)}, f32[256,1536]{1,0:T(8,128)S(1)}, u32[]{:S(2)}) copy-start(f32[256,1536]{1,0:T(8,128)S(1)} %get-tuple-element.60) | copy-start | bytes 4718596
  215.2 2.8 copy-start.13
  215.2 2.8 copy-start.14
  215.2 2.8 copy-start.15
  226.7 43.1 %all-to-all-start.4 = ((f32[1,128,4608]{2,0,1:T(1,128)}), f32[1,128,4608]{2,0,1:T(1,128)S(1)}, u32[]{:S(2)}, u32[]{:S(2)}) async-start(f32[1,128,4608]{2,0,1:T(1,128)} %copy.95), calls=%async_computation.4 | async-start | bytes 4718592 | tf_op jit(solution)/shard_map/all_to_all | solution.py:160
  455.5 7.0 %copy-start.1 = (bf16[16,1536]{1,0:T(8,128)(2,1)S(1)}, bf16[16,1536]{1,0:T(8,128)(2,1)}, u32[]{:S(2)}) copy-start(bf16[16,1536]{1,0:T(8,128)(2,1)} %param.17) | copy-start | bytes 147460
Sparse Core Ops, SparseCore 0:
  215.3 240.1 all-reduce.6
where the time goes:
time: 474 us; the launch traced here: 470 us
  waiting for transfers between devices  244 us (51%)
  blocking collectives  68.6 us (14%)
  other arithmetic  47.5 us (10%)
  local copies, waits for them, and re-layouts  32.4 us (7%)
  matrix products  29.6 us (6%)
  starting transfers between devices  29.4 us (6%)
  between operations  18 us (4%)
    unnamed x2, waiting for transfers between devices  174 us
    unnamed x1, blocking collectives  68.6 us
    all_to_all x1, waiting for transfers between devices, body(): lax.all_to_all(returning, ('seq', 'head'), split_axis=1, concat_axis=1, t...  38.2 us
    all_to_all x1, waiting for transfers between devices, body(): lax.all_to_all(outgoing[0], ('seq', 'head'), split_axis=1, concat_axis=1,...  18.4 us
    dot_general x4, matrix products, contract_rows(): lax.dot_general(left_rows, right_rows, (((0,), (0,)), ((), ())), preferre...  15 us
    unnamed x56, local copies, waits for them, and re-layouts  14.5 us
    concatenate x1, other arithmetic, body(): jnp.concatenate([first_part, second_part], axis=1)  12.6 us
    all_to_all x1, starting transfers between devices, body(): lax.all_to_all(outgoing[0], ('seq', 'head'), split_axis=1, concat_axis=1,...  9.77 us
  transfers between devices with their start and end apart: 6, of which 5 were waited for; matrix products, arithmetic and copies ran while one was open for 10% of the time, Pallas kernels for 0%

commit v1 on v0

v1 whole, which is shorter than its diff:
```python
import jax
import jax.numpy as jnp
from jax import lax
from jax.experimental import pallas as pl
from jax.experimental.pallas import tpu as pltpu
from jax.sharding import PartitionSpec as P

f32, bf16 = jnp.float32, jnp.bfloat16
EPS = 1e-6
W, C, DRAWS, ROWS, NB = 1536, 16, 4, 128, 256
R = DRAWS * ROWS
NT = (((1,), (1,)), ((), ()))
TN = (((0,), (0,)), ((), ()))


def dot(a, b):
    return jnp.dot(a, b, preferred_element_type=f32)


def dot_nt(a, b):
    return lax.dot_general(a, b, NT, preferred_element_type=f32)


def dot_tn(a, b):
    return lax.dot_general(a, b, TN, preferred_element_type=f32)


def columns(j, base=0):
    return pl.ds(pl.multiple_of(base + j * NB, NB), NB)


def make_noisy(lat, noise, times, noisy_s, nd_s):
    ang = (0.5 * jnp.pi) * times[...].astype(f32)
    cosv, sinv = jnp.cos(ang), jnp.sin(ang)
    latv = lat[...].astype(f32)
    for k in range(DRAWS):
        nz = noise[:, C * k:C * (k + 1)].astype(f32)
        noisy_s[k * ROWS:(k + 1) * ROWS, :] = (cosv[:, k:k + 1] * latv + sinv[:, k:k + 1] * nz).astype(bf16)
        nd_s[k * ROWS:(k + 1) * ROWS, :] = nz


def stream(noisy_s, inw, st_s):
    @pl.loop(0, W // NB)
    def _(j):
        st_s[:, columns(j)] = dot(noisy_s[...], inw[:, columns(j)])


def norm_in(mod, st_s, ni_s, ri_s, bi_s):
    @pl.loop(0, ROWS // 16)
    def _(i):
        t0 = pl.multiple_of(i * 16, 16)
        t = pl.ds(t0, 16)
        for k in range(DRAWS):
            r = pl.ds(pl.multiple_of(k * ROWS + t0, 16), 16)
            x = st_s[r, :]
            c = x - jnp.mean(x, axis=-1, keepdims=True)
            rs = lax.rsqrt(jnp.mean(c * c, axis=-1, keepdims=True) + EPS)
            n = c * rs
            ni_s[r, :] = n
            ri_s[r, :] = rs
            bi_s[r, :] = (n * (1.0 + mod[t, W:2 * W].astype(f32)) + mod[t, 0:W].astype(f32)).astype(bf16)


def fc1_fwd(bi_s, fc1, h_s, d_s):
    @pl.loop(0, W // NB)
    def _(j):
        hp = dot(bi_s[...], fc1[:, columns(j)])
        sg = jax.nn.sigmoid(hp)
        h_s[:, columns(j)] = (hp * sg).astype(bf16)
        d_s[:, columns(j)] = sg * (1.0 + hp * (1.0 - sg))


def fc2_fwd(mod, h_s, fc2, st_s, bo_s):
    @pl.loop(0, W // NB)
    def _(j):
        bo = dot(h_s[...], fc2[:, columns(j)])
        bo_s[:, columns(j)] = bo
        gate = mod[:, columns(j, 2 * W)].astype(f32)
        for k in range(DRAWS):
            r = slice(k * ROWS, (k + 1) * ROWS)
            st_s[r, columns(j)] = st_s[r, columns(j)] + gate * bo[r]


def norm_out(st_s, ro_s, fin_s):
    @pl.loop(0, R // 32)
    def _(i):
        r = pl.ds(pl.multiple_of(i * 32, 32), 32)
        x = st_s[r, :]
        c = x - jnp.mean(x, axis=-1, keepdims=True)
        rs = lax.rsqrt(jnp.mean(c * c, axis=-1, keepdims=True) + EPS)
        n = c * rs
        st_s[r, :] = n
        ro_s[r, :] = rs
        fin_s[r, :] = n.astype(bf16)


def predict(cnt, fin_s, outw, nd_s, pd_s, m1_s, m2_s):
    pred = dot_nt(fin_s[...], outw[...])
    ows = dot_nt(jnp.ones((8, W), bf16), outw[...])[0:1, :] * (1.0 / W)
    tok = lax.broadcasted_iota(jnp.int32, (R, 1), 0) & (ROWS - 1)
    live = (tok < cnt[0]).astype(f32)
    pd = (2.0 * (pred - nd_s[...]) * live).astype(bf16)
    pd_s[...] = pd
    pf = pd.astype(f32)
    m1_s[...] = jnp.sum(pf * ows, axis=-1, keepdims=True)
    m2_s[...] = jnp.sum(pf * pred, axis=-1, keepdims=True) * (1.0 / W)


def stream_grad(mod, pd_s, outw, st_s, ro_s, m1_s, m2_s, bo_s, sg_s, bg_s, mod_out):
    @pl.loop(0, W // NB)
    def _(j):
        fg = dot(pd_s[...], outw[:, columns(j)])
        gate = mod[:, columns(j, 2 * W)].astype(f32)
        acc = None
        for k in range(DRAWS):
            r = slice(k * ROWS, (k + 1) * ROWS)
            sg = ro_s[r, :] * (fg[r] - m1_s[r, :] - st_s[r, columns(j)] * m2_s[r, :])
            sg_s[r, columns(j)] = sg
            bg_s[r, columns(j)] = (sg * gate).astype(bf16)
            t = sg * bo_s[r, columns(j)]
            acc = t if acc is None else acc + t
        mod_out[:, columns(j, 2 * W)] = acc


def pre_grad(bg_s, fc2, d_s, pg_s):
    @pl.loop(0, W // NB)
    def _(j):
        ag = dot_nt(bg_s[...], fc2[columns(j), :])
        pg_s[:, columns(j)] = (ag * d_s[:, columns(j)]).astype(bf16)


def block_grad(mod, pg_s, fc1, ni_s, blk_s, a1_s, a2_s, mod_out):
    a1_s[...] = jnp.zeros_like(a1_s)
    a2_s[...] = jnp.zeros_like(a2_s)

    @pl.loop(0, W // NB)
    def _(j):
        blk = dot_nt(pg_s[...], fc1[columns(j), :])
        sp = 1.0 + mod[:, columns(j, W)].astype(f32)
        s0 = s1 = None
        for k in range(DRAWS):
            r = slice(k * ROWS, (k + 1) * ROWS)
            n = ni_s[r, columns(j)]
            b = blk[r]
            bn = b * n
            g = b * sp
            blk_s[r, columns(j)] = g
            gn = g * n
            a1_s[r, :] = a1_s[r, :] + (g[:, :128] + g[:, 128:])
            a2_s[r, :] = a2_s[r, :] + (gn[:, :128] + gn[:, 128:])
            s0 = b if s0 is None else s0 + b
            s1 = bn if s1 is None else s1 + bn
        mod_out[:, columns(j)] = s0
        mod_out[:, columns(j, W)] = s1


def input_grad(ri_s, ni_s, sg_s, blk_s, a1_s, a2_s, ib_s):
    a1_s[:, 0:1] = jnp.sum(a1_s[...], axis=-1, keepdims=True) * (1.0 / W)
    a2_s[:, 0:1] = jnp.sum(a2_s[...], axis=-1, keepdims=True) * (1.0 / W)

    @pl.loop(0, R // 32)
    def _(i):
        r = pl.ds(pl.multiple_of(i * 32, 32), 32)
        v = sg_s[r, :] + ri_s[r, :] * (blk_s[r, :] - a1_s[r, 0:1] - ni_s[r, :] * a2_s[r, 0:1])
        ib_s[r, :] = v.astype(bf16)


def edges(noisy_s, ib_s, pd_s, fin_s, e_out):
    e_out[0:C, :] = dot_tn(noisy_s[...], ib_s[...])
    e_out[C:2 * C, :] = dot_tn(pd_s[...], fin_s[...])


def local_kernel(cnt, mod, lat, noise, times, inw, fc1, fc2, outw,
                 mod_out, h_s, bg_s, bi_s, pg_s, e_out,
                 noisy_s, nd_s, st_s, ni_s, ri_s, d_s, bo_s, ro_s, fin_s, pd_s, m1_s, m2_s,
                 sg_s, blk_s, a1_s, a2_s, ib_s):
    make_noisy(lat, noise, times, noisy_s, nd_s)
    stream(noisy_s, inw, st_s)
    norm_in(mod, st_s, ni_s, ri_s, bi_s)
    fc1_fwd(bi_s, fc1, h_s, d_s)
    fc2_fwd(mod, h_s, fc2, st_s, bo_s)
    norm_out(st_s, ro_s, fin_s)
    predict(cnt, fin_s, outw, nd_s, pd_s, m1_s, m2_s)
    stream_grad(mod, pd_s, outw, st_s, ro_s, m1_s, m2_s, bo_s, sg_s, bg_s, mod_out)
    pre_grad(bg_s, fc2, d_s, pg_s)
    block_grad(mod, pg_s, fc1, ni_s, blk_s, a1_s, a2_s, mod_out)
    input_grad(ri_s, ni_s, sg_s, blk_s, a1_s, a2_s, ib_s)
    edges(noisy_s, ib_s, pd_s, fin_s, e_out)


def local_call(mod, lat, noise, times, cnt, inw, fc1, fc2, outw):
    v = pl.BlockSpec(memory_space=pltpu.VMEM)
    S = lambda s, d=f32: pltpu.VMEM(s, d)
    O = jax.ShapeDtypeStruct
    return pl.pallas_call(
        local_kernel,
        out_shape=[O((ROWS, 3 * W), f32)] + [O((R, W), bf16)] * 4 + [O((2 * C, W), f32)],
        in_specs=[pl.BlockSpec(memory_space=pltpu.SMEM)] + [v] * 8,
        out_specs=[v] * 6,
        scratch_shapes=[S((R, C), bf16), S((R, C)), S((R, W)), S((R, W)), S((R, 1)), S((R, W)), S((R, W)), S((R, 1)),
                        S((R, W), bf16), S((R, C), bf16), S((R, 1)), S((R, 1)), S((R, W)), S((R, W)), S((R, 128)),
                        S((R, 128)), S((R, W), bf16)],
        compiler_params=pltpu.CompilerParams(vmem_limit_bytes=60 * 1024 * 1024),
        cost_estimate=pl.CostEstimate(flops=8 * R * W * W, bytes_accessed=20_000_000, transcendentals=R * W),
    )(cnt, mod, lat, noise, times, inw, fc1, fc2, outw)


MESH = pl.DeviceIdType.MESH
ORDER = (("y", "z", "x"), ("z", "x", "y"), ("x", "y", "z"))
HALF, PART, PIECE = W // 2, W // 6, 24
FACTOR = (ROWS * 128 // 2) ** -0.5


def place():
    s, h = lax.axis_index("seq"), lax.axis_index("head")
    return {"y": lax.div(s, 4), "z": lax.rem(s, 4), "x": lax.div(h, 2)}, lax.rem(h, 2)


def away(pos, axis, d):
    out = dict(pos)
    out[axis] = lax.rem(pos[axis] + d, 4)
    return out


def device(pos, core):
    return (pos["y"] * 4 + pos["z"], pos["x"] * 2 + core)


def remote(src, dst, ssem, rsem, dev):
    return pltpu.make_async_remote_copy(
        src_ref=src, dst_ref=dst, send_sem=ssem, recv_sem=rsem, device_id=dev, device_id_type=MESH)


def greet(pos, core):
    barrier = pltpu.get_barrier_semaphore()
    peers = [device(pos, 1 - core)]
    for axis in ("y", "z", "x"):
        for d in (1, 2, 3):
            peers.append(device(away(pos, axis, d), core))
    for dev in peers:
        pl.semaphore_signal(barrier, inc=1, device_id=dev, device_id_type=MESH)
    pl.semaphore_wait(barrier, len(peers))


class Ring:
    def __init__(self, pos, core, axis, buf, got, ssem, rsem):
        self.a0 = pos[axis]
        self.buf, self.got = buf, got
        up, down = device(away(pos, axis, 1), core), device(away(pos, axis, 3), core)
        far, nxt, prv = (lax.rem(self.a0 + d, 4) for d in (2, 1, 3))
        self.nxt, self.prv = nxt, prv
        route = ((far, 0, up), (far, 1, down), (nxt, 1, up), (prv, 0, down), (nxt, 0, up), (prv, 1, down))
        self.copies = [
            remote(buf.at[k, half], got.at[i], ssem.at[i], rsem.at[i], dev) for i, (k, half, dev) in enumerate(route)]

    def start(self):
        for c in self.copies[:4]:
            c.start()

    def relay(self):
        for i, k, half in ((0, self.nxt, 0), (1, self.prv, 1)):
            self.copies[i].wait_recv()
            total = self.buf[k, half].astype(f32) + self.got[i].astype(f32)
            self.buf[k, half] = total.astype(bf16)
            self.copies[4 + i].start()

    def finish(self):
        for i in (2, 3, 4, 5):
            self.copies[i].wait_recv()
        sums = []
        for half, i, j in ((0, 4, 3), (1, 2, 5)):
            sums.append(self.buf[self.a0, half].astype(f32) + self.got[i].astype(f32) + self.got[j].astype(f32))
        return sums

    def drain(self):
        for c in self.copies:
            c.wait_send()


def weight_part(p, left, left_r, right, right_r, core, g_s, out):
    own = pl.ds(pl.multiple_of(core * HALF + p * PART, PART), PART)
    theirs = pl.ds(p * PART, PART)

    @pl.loop(0, 4)
    def _(i):
        rows = pl.ds(pl.multiple_of(i * 384, 384), 384)
        g = dot_tn(left[:, rows], right[:, own]) + dot_tn(left_r[:, rows], right_r[:, theirs])
        if p == 0:
            for half in range(2):
                out[i, half] = g[half * 192:(half + 1) * 192].astype(bf16)
        else:
            g_s[i] = g

    def piece(y, z, x):
        return g_s[y, (z * 4 + x) * PIECE:(z * 4 + x + 1) * PIECE, :]

    if p > 0:
        for a in range(4):
            for b in range(4):
                rows = [piece(c, a, b) if p == 1 else piece(b, c, a) for c in range(4)]
                out[a, b // 2, (b % 2) * 96:(b % 2 + 1) * 96] = jnp.concatenate(rows, axis=0).astype(bf16)


def scatter_kernel(h, bg, bi, pg, e, fc1_out, fc2_out, in_out, out_out,
                   h_r, bg_r, bi_r, pg_r, g_s, s1, r1, s2, r2, q_s, u_s, v_s, w_s, x_s,
                   e_r, ey_s, ey_r, ez_s, ez_r, ex_s, ex_r,
                   pair_ss, pair_rs, ss1, rs1, ss2, rs2, ss3, rs3, ess, ers):
    pos, core = place()
    greet(pos, core)
    other = device(pos, 1 - core)
    theirs = pl.ds(pl.multiple_of((1 - core) * HALF, HALF), HALF)
    pair = [remote(src, dst, pair_ss.at[i], pair_rs.at[i], other) for i, (src, dst) in enumerate(
        ((h, h_r), (bg.at[:, theirs], bg_r), (bi, bi_r), (pg.at[:, theirs], pg_r), (e, e_r)))]
    for c in pair:
        c.start()
    rings1 = [[Ring(pos, core, ORDER[p][0], s1.at[m, p], r1.at[m, p], ss1.at[m, p], rs1.at[m, p])
               for p in range(3)] for m in range(2)]
    rings2 = [[Ring(pos, core, ORDER[p][1], s2.at[m, p], r2.at[m, p], ss2.at[m, p], rs2.at[m, p])
               for p in range(3)] for m in range(2)]
    side = {}

    def edge_start(axis, src, dst, base):
        side[axis] = []
        for d in (1, 2, 3):
            k = lax.rem(pos[axis] + d, 4)
            s = src.at[k] if axis == "y" else src
            c = remote(s, dst.at[d - 1], ess.at[base + d - 1], ers.at[base + d - 1], device(away(pos, axis, d), core))
            c.start()
            side[axis].append(c)

    def edge_finish(axis, mine, dst):
        for c in side[axis]:
            c.wait_recv()
        return mine + dst[0] + dst[1] + dst[2]

    def pass1(m, left, left_r, right, right_r):
        for p in range(3):
            weight_part(p, left, left_r, right, right_r, core, g_s, s1.at[m, p])
            rings1[m][p].start()

    def pass2(m):
        for p in range(3):
            for hb, v in enumerate(rings1[m][p].finish()):
                v = v.astype(bf16)
                for b in range(2):
                    for hc in range(2):
                        at = (b * 2 + hc) * 48
                        s2[m, p, 2 * hb + b, hc] = v[at:at + 48]
            rings2[m][p].start()

    def pass3(m):
        for p in range(3):
            for hc, v in enumerate(rings2[m][p].finish()):
                for c in range(2):
                    q_s[p, 2 * hc + c, m * PIECE:(m + 1) * PIECE, :] = v[c * PIECE:(c + 1) * PIECE]

    pair[0].wait_recv()
    pair[1].wait_recv()
    pass1(0, h, h_r, bg, bg_r)
    pair[4].wait_recv()
    for k in range(4):
        ey_s[k] = e[:, k * 384:(k + 1) * 384] + e_r[:, k * 384:(k + 1) * 384]
    edge_start("y", ey_s, ey_r, 0)
    for p in range(3):
        rings1[0][p].relay()
    pair[2].wait_recv()
    pair[3].wait_recv()
    pass1(1, bi, bi_r, pg, pg_r)
    ez_s[...] = edge_finish("y", ey_s[pos["y"]], ey_r)
    edge_start("z", ez_s, ez_r, 3)
    pass2(0)
    for p in range(3):
        rings1[1][p].relay()
    for p in range(3):
        rings2[0][p].relay()
    ex_s[...] = edge_finish("z", ez_s[...], ez_r)
    edge_start("x", ex_s, ex_r, 6)
    pass3(0)
    pass2(1)
    ee = edge_finish("x", ex_s[...], ex_r) * FACTOR
    q = pos["z"] * 8 + pos["x"] * 2 + core
    ee = pltpu.roll(ee, lax.rem(384 - 12 * q, 384), 1)
    in_out[...] = ee[0:C, 0:12]
    out_out[...] = ee[C:2 * C, 0:12]
    for p in range(3):
        rings2[1][p].relay()
    pass3(1)
    last = []
    for p in range(3):
        axis = ORDER[p][2]
        u_s[p] = q_s[p].astype(bf16)
        for d in (1, 2, 3):
            k = lax.rem(pos[axis] + d, 4)
            c = remote(u_s.at[p, k], v_s.at[p, d - 1], ss3.at[p, d - 1], rs3.at[p, d - 1], device(away(pos, axis, d), core))
            c.start()
            last.append(c)
    for p in range(3):
        for c in last[3 * p:3 * p + 3]:
            c.wait_recv()
        tot = q_s[p, pos[ORDER[p][2]]]
        for d in range(3):
            tot = tot + v_s[p, d].astype(f32)
        w_s[:, p * PART:(p + 1) * PART] = tot * FACTOR
    final = remote(w_s, x_s, pair_ss.at[5], pair_rs.at[5], other)
    final.start()
    mine = pl.ds(pl.multiple_of(core * HALF, HALF), HALF)
    final.wait_recv()
    for m, out in ((0, fc2_out), (1, fc1_out)):
        for src, cols in ((w_s, mine), (x_s, theirs)):
            v = src[m * PIECE:(m + 1) * PIECE, :]
            out[:, cols] = jnp.where(core == 0, v[0:12], v[12:24])
    for m in range(2):
        for p in range(3):
            rings1[m][p].drain()
            rings2[m][p].drain()
    for c in pair + last + side["y"] + side["z"] + side["x"] + [final]:
        c.wait_send()


def scatter_call(h, bg, bi, pg, e):
    v = pl.BlockSpec(memory_space=pltpu.VMEM)
    O = jax.ShapeDtypeStruct
    V = pltpu.VMEM
    D = pltpu.SemaphoreType.DMA
    return pl.pallas_call(
        scatter_kernel,
        out_shape=[O((12, W), f32), O((12, W), f32), O((C, 12), f32), O((C, 12), f32)],
        in_specs=[v] * 5,
        out_specs=[v] * 4,
        scratch_shapes=[
            V((R, W), bf16), V((R, HALF), bf16), V((R, W), bf16), V((R, HALF), bf16), V((4, 384, PART), f32),
            V((2, 3, 4, 2, 192, PART), bf16), V((2, 3, 6, 192, PART), bf16),
            V((2, 3, 4, 2, 48, PART), bf16), V((2, 3, 6, 48, PART), bf16),
            V((3, 4, 48, PART), f32), V((3, 4, 48, PART), bf16), V((3, 3, 48, PART), bf16),
            V((48, HALF), f32), V((48, HALF), f32),
            V((2 * C, W), f32), V((4, 2 * C, 384), f32), V((3, 2 * C, 384), f32),
            V((2 * C, 384), f32), V((3, 2 * C, 384), f32), V((2 * C, 384), f32), V((3, 2 * C, 384), f32),
            D((6,)), D((6,)), D((2, 3, 6)), D((2, 3, 6)), D((2, 3, 6)), D((2, 3, 6)), D((3, 3)), D((3, 3)), D((9,)), D((9,)),
        ],
        compiler_params=pltpu.CompilerParams(
            collective_id=0, has_side_effects=True, vmem_limit_bytes=56 * 1024 * 1024),
        cost_estimate=pl.CostEstimate(flops=4 * R * W * W, bytes_accessed=10_000_000, transcendentals=0),
    )(h, bg, bi, pg, e)


def body(modulation, latents, noise, times, image_rows, in_weight, fc1_weight, fc2_weight, out_weight):
    mod_grad, h, bg, bi, pg, e = local_call(
        modulation, latents, noise, times, image_rows, in_weight, fc1_weight, fc2_weight, out_weight)
    fc1_grad, fc2_grad, in_grad, out_grad = scatter_call(h, bg, bi, pg, e)
    return mod_grad, fc1_grad, fc2_grad, in_grad, out_grad


def solution(mesh):
    rows = P(("seq", "head"), None)
    cols = P(None, ("seq", "head"))
    return jax.shard_map(
        body, mesh=mesh, in_specs=(rows, rows, rows, rows, P(("seq", "head")), P(), P(), P(), P()),
        out_specs=(rows, rows, rows, cols, cols), check_vma=False)
```

time: 474 us -> 103 us (0.22)
  waiting for transfers between devices: 244 us -> 0 us
  Pallas kernels: 0 us -> 91.9 us
  blocking collectives: 68.6 us -> 0 us
  other arithmetic: 47.5 us -> 0 us
  matrix products: 29.6 us -> 0 us
  starting transfers between devices: 29.4 us -> 0 us
  local copies, waits for them, and re-layouts: 32.4 us -> 9.89 us
  between operations: 18 us -> 1.29 us
    unnamed x2 -> x0, waiting for transfers between devices: 174 us -> none
    pallas_call x0 -> x2, Pallas kernels: none -> 91.9 us  [the longest x1 57.9 us: scatter_call(): pl.pallas_call(scatter_kernel, out_shape=[O((12, W), f32), O((12, W), f32...]
    all_to_all x5 -> x0, waiting for transfers between devices: 69.5 us -> none  [the longest x1 38.2 us: body(): lax.all_to_all(returning, ('seq', 'head'), split_axis=1, concat_axis=1, t...]
    unnamed x1 -> x0, blocking collectives: 68.6 us -> none
    dot_general x11 -> x0, matrix products: 29.6 us -> none  [the longest x4 15 us: contract_rows(): lax.dot_general(left_rows, right_rows, (((0,), (0,)), ((), ())), preferre...]
    all_to_all x5 -> x0, starting transfers between devices: 29.3 us -> none  [the longest x1 9.77 us: body(): lax.all_to_all(outgoing[0], ('seq', 'head'), split_axis=1, concat_axis=1,...]
    concatenate x7 -> x0, other arithmetic: 26.3 us -> none  [the longest x1 12.6 us: body(): jnp.concatenate([first_part, second_part], axis=1)]
    gather x11 -> x0, local copies, waits for them, and re-layouts: 9.23 us -> none  [the longest x7 3.08 us: body(): jnp.take(member, slot_index, axis=0)]
  transfers between devices with their start and end apart: 6 -> 0, of which waited for: 5 -> 0; matrix products, arithmetic and copies ran while one was open for 10% -> 0% of each run, Pallas kernels for 0% -> 0%
where the time goes in v1:
time: 103 us
  Pallas kernels  91.9 us (89%)
  local copies, waits for them, and re-layouts  9.89 us (10%)
  between operations  1.29 us (1%)
    pallas_call x1, Pallas kernels, scatter_call(): pl.pallas_call(scatter_kernel, out_shape=[O((12, W), f32), O((12, W), f32...  57.9 us
    pallas_call x1, Pallas kernels, local_call(): pl.pallas_call(local_kernel, out_shape=[O((ROWS, 3 * W), f32)] + [O((R, W...  34 us
    unnamed x7, local copies, waits for them, and re-layouts  9.89 us

profile of v1, /device:TPU:1, one launch (start us, length us, event | category | flops | bytes accessed | tf_op | source)
XLA Modules:
  0.0 103.1 jit_solution(12446067976539520750)
XLA Ops:
  1.3 1.4 %copy.14.lat = bf16[128,16]{1,0:T(8,128)(2,1)} copy(bf16[128,16]{0,1:T(8,128)(2,1)} %param.10) | data formatting | bytes 8192 | tf_op args[1]
  2.7 1.4 %copy.15.noise = bf16[128,64]{1,0:T(8,128)(2,1)} copy(bf16[128,64]{0,1:T(8,128)(2,1)} %param.11) | data formatting | bytes 32768 | tf_op args[2]
  4.1 1.4 %copy.16.times = bf16[128,4]{1,0:T(8,128)(2,1)} copy(bf16[128,4]{0,1:T(4,128)(2,1)} %param.12) | data formatting | bytes 2048 | tf_op args[3]
  5.5 34.0 %shard_map.128 = (f32[128,4608]{1,0:T(8,128)}, bf16[512,1536]{1,0:T(8,128)(2,1)}, bf16[512,1536]{1,0:T(8,128)(2,1)}, bf16[512,1536]{1,0:T(8,128)(2,1)}, bf16[512,1536]{1,0:T(8,128)(2,1)}, /*index=5*/f32[32,1536]{1,0:T(8,128)}) custom-call(s32[1]{0:T(128)S(6)} %copy.21.cnt, bf16[128,4608]{1,0:T(8,128)(2,1)} %mod.1, bf16[128,16]{1,0:T(8,128)(2,1)} %copy.14.lat, ...), custom_call_target="tpu_custom_call" | custom-call | flops 9663676416 | bytes 20000000 | tf_op jit(solution)/shard_map/pallas_call | solution.py:195
  39.5 57.9 %shard_map.129 = (f32[12,1536]{1,0:T(8,128)}, f32[12,1536]{1,0:T(8,128)}, f32[16,12]{1,0:T(8,128)}, f32[16,12]{1,0:T(8,128)}) custom-call(bf16[512,1536]{1,0:T(8,128)(2,1)} %get-tuple-element.16.h, bf16[512,1536]{1,0:T(8,128)(2,1)} %get-tuple-element.17.bg, bf16[512,1536]{1,0:T(8,128)(2,1)} %get-tuple-element.18.bi, bf16[512,1536]{1,0:T(8,128)(2,1)} %get-tuple-element.19.pg, ...), custom_call_target="tpu_custom_call" | custom-call | flops 4831838208 | bytes 10000000 | tf_op jit(solution)/shard_map/pallas_call | solution.py:425
  97.4 1.5 %copy.22 = f32[12,1536]{1,0:T(8,128)} copy(f32[12,1536]{1,0:T(8,128)} %get-tuple-element.31) | data formatting | bytes 147456
  98.9 1.5 %copy.23 = f32[12,1536]{1,0:T(8,128)} copy(f32[12,1536]{1,0:T(8,128)} %get-tuple-element.32) | data formatting | bytes 147456
  100.5 1.3 %copy.24 = f32[16,12]{1,0:T(8,128)} copy(f32[16,12]{1,0:T(8,128)} %get-tuple-element.33) | data formatting | bytes 1536
  101.8 1.3 %copy.25 = f32[16,12]{1,0:T(8,128)} copy(f32[16,12]{1,0:T(8,128)} %get-tuple-element.34) | data formatting | bytes 1536

commit v2 on v1

v2 whole, which is shorter than its diff:
```python
import jax
import jax.numpy as jnp
from jax import lax
from jax.experimental import pallas as pl
from jax.experimental.pallas import tpu as pltpu
from jax.sharding import PartitionSpec as P

f32, bf16 = jnp.float32, jnp.bfloat16
EPS = 1e-6
W, C, DRAWS, ROWS, NB = 1536, 16, 4, 128, 256
R = DRAWS * ROWS
NT = (((1,), (1,)), ((), ()))
TN = (((0,), (0,)), ((), ()))


def dot(a, b):
    return jnp.dot(a, b, preferred_element_type=f32)


def dot_nt(a, b):
    return lax.dot_general(a, b, NT, preferred_element_type=f32)


def dot_tn(a, b):
    return lax.dot_general(a, b, TN, preferred_element_type=f32)


def columns(j, base=0):
    return pl.ds(pl.multiple_of(base + j * NB, NB), NB)


def draw(k):
    return slice(k * ROWS, (k + 1) * ROWS)


def make_noisy(lat, noise, times, noisy_s):
    ang = (0.5 * jnp.pi) * times[...].astype(f32)
    cosv, sinv = jnp.cos(ang), jnp.sin(ang)
    latv = lat[...].astype(f32)
    for k in range(DRAWS):
        nz = noise[C * k:C * (k + 1), :].astype(f32)
        noisy_s[:, draw(k)] = (cosv[k:k + 1, :] * latv + sinv[k:k + 1, :] * nz).astype(bf16)


def stream(noisy_s, inw, st_s):
    @pl.loop(0, W // NB)
    def _(j):
        st_s[:, columns(j)] = dot_tn(noisy_s[...], inw[:, columns(j)])


def norm_in(mod, st_s, ni_s, ri_s, bi_s):
    @pl.loop(0, ROWS // 16)
    def _(i):
        t0 = pl.multiple_of(i * 16, 16)
        t = pl.ds(t0, 16)
        for k in range(DRAWS):
            r = pl.ds(pl.multiple_of(k * ROWS + t0, 16), 16)
            x = st_s[r, :]
            c = x - jnp.mean(x, axis=-1, keepdims=True)
            rs = lax.rsqrt(jnp.mean(c * c, axis=-1, keepdims=True) + EPS)
            n = c * rs
            ni_s[r, :] = n
            ri_s[r, :] = rs
            bi_s[r, :] = (n * (1.0 + mod[t, W:2 * W].astype(f32)) + mod[t, 0:W].astype(f32)).astype(bf16)


def fc1_fwd(bi_s, fc1, h_s, d_s):
    @pl.loop(0, W // NB)
    def _(j):
        hp = dot(bi_s[...], fc1[:, columns(j)])
        sg = jax.nn.sigmoid(hp)
        h_s[:, columns(j)] = (hp * sg).astype(bf16)
        d_s[:, columns(j)] = sg * (1.0 + hp * (1.0 - sg))


def fc2_fwd(mod, h_s, fc2, st_s, bo_s):
    @pl.loop(0, W // NB)
    def _(j):
        bo = dot(h_s[...], fc2[:, columns(j)])
        bo_s[:, columns(j)] = bo
        gate = mod[:, columns(j, 2 * W)].astype(f32)
        for k in range(DRAWS):
            st_s[draw(k), columns(j)] = st_s[draw(k), columns(j)] + gate * bo[draw(k)]


def norm_out(st_s, ro_s, fin_s):
    @pl.loop(0, R // 32)
    def _(i):
        r = pl.ds(pl.multiple_of(i * 32, 32), 32)
        x = st_s[r, :]
        c = x - jnp.mean(x, axis=-1, keepdims=True)
        rs = lax.rsqrt(jnp.mean(c * c, axis=-1, keepdims=True) + EPS)
        n = c * rs
        st_s[r, :] = n
        ro_s[r, :] = rs
        fin_s[r, :] = n.astype(bf16)


def predict(cnt, noise, fin_s, outw, pd_s, m_s):
    pred = dot_nt(outw[...], fin_s[...])
    ows = jnp.sum(outw[...].astype(f32), axis=-1, keepdims=True) * (1.0 / W)
    live = (lax.broadcasted_iota(jnp.int32, (1, ROWS), 1) < cnt[0]).astype(f32)
    for k in range(DRAWS):
        p = pred[:, draw(k)]
        pd = (2.0 * (p - noise[C * k:C * (k + 1), :].astype(f32)) * live).astype(bf16)
        pd_s[:, draw(k)] = pd
        pf = pd.astype(f32)
        m1 = jnp.sum(pf * ows, axis=0, keepdims=True)
        m2 = jnp.sum(pf * p, axis=0, keepdims=True) * (1.0 / W)
        m = jnp.concatenate([m1, m2, jnp.zeros((6, ROWS), f32)], axis=0)
        m_s[draw(k), :] = m.T


def stream_grad(mod, pd_s, outw, st_s, ro_s, m_s, bo_s, bg_s, mod_out, order, span):
    @pl.loop(*span)
    def _(i):
        j = order(i)
        fg = dot_tn(pd_s[...], outw[:, columns(j)])
        gate = mod[:, columns(j, 2 * W)].astype(f32)
        acc = None
        for k in range(DRAWS):
            r = draw(k)
            sg = ro_s[r, :] * (fg[r] - m_s[r, 0:1] - st_s[r, columns(j)] * m_s[r, 1:2])
            bg_s[r, columns(j)] = (sg * gate).astype(bf16)
            t = sg * bo_s[r, columns(j)]
            bo_s[r, columns(j)] = sg
            acc = t if acc is None else acc + t
        mod_out[:, columns(j, 2 * W)] = acc


def pre_grad(bg_s, fc2, d_s, pg_s, order, span):
    @pl.loop(*span)
    def _(i):
        j = order(i)
        ag = dot_nt(bg_s[...], fc2[columns(j), :])
        pg_s[:, columns(j)] = (ag * d_s[:, columns(j)]).astype(bf16)


def block_grad(mod, pg_s, fc1, ni_s, blk_s, a1_s, a2_s, mod_out, span):
    @pl.loop(*span)
    def _(j):
        blk = dot_nt(pg_s[...], fc1[columns(j), :])
        sp = 1.0 + mod[:, columns(j, W)].astype(f32)
        s0 = s1 = None
        for k in range(DRAWS):
            r = draw(k)
            n = ni_s[r, columns(j)]
            b = blk[r]
            bn = b * n
            g = b * sp
            blk_s[r, columns(j)] = g
            gn = g * n
            a1_s[r, :] = a1_s[r, :] + (g[:, :128] + g[:, 128:])
            a2_s[r, :] = a2_s[r, :] + (gn[:, :128] + gn[:, 128:])
            s0 = b if s0 is None else s0 + b
            s1 = bn if s1 is None else s1 + bn
        mod_out[:, columns(j)] = s0
        mod_out[:, columns(j, W)] = s1


def input_grad(ri_s, ni_s, sg_s, blk_s, a1_s, a2_s, ib_s):
    @pl.loop(0, R // 32)
    def _(i):
        r = pl.ds(pl.multiple_of(i * 32, 32), 32)
        m1 = jnp.sum(a1_s[r, :], axis=-1, keepdims=True) * (1.0 / W)
        m2 = jnp.sum(a2_s[r, :], axis=-1, keepdims=True) * (1.0 / W)
        v = sg_s[r, :] + ri_s[r, :] * (blk_s[r, :] - m1 - ni_s[r, :] * m2)
        ib_s[r, :] = v.astype(bf16)


MESH = pl.DeviceIdType.MESH
ORDER = (("y", "z", "x"), ("z", "x", "y"), ("x", "y", "z"))
HALF, PART, PIECE = W // 2, W // 6, 24
FACTOR = (ROWS * 128 // 2) ** -0.5
SEQ, HEAD = 16, 8
GROUP = W // SEQ


def place():
    s, h = lax.axis_index("seq"), lax.axis_index("head")
    return {"y": lax.div(s, 4), "z": lax.rem(s, 4), "x": lax.div(h, 2)}, lax.rem(h, 2)


def away(pos, axis, d):
    out = dict(pos)
    out[axis] = lax.rem(pos[axis] + d, 4)
    return out


def device(pos, core):
    return (pos["y"] * 4 + pos["z"], pos["x"] * 2 + core)


def remote(src, dst, ssem, rsem, dev):
    return pltpu.make_async_remote_copy(
        src_ref=src, dst_ref=dst, send_sem=ssem, recv_sem=rsem, device_id=dev, device_id_type=MESH)


def peers(pos, core):
    s, h = lax.axis_index("seq"), lax.axis_index("head")
    out = [(lax.rem(s + d, SEQ), h) for d in range(1, SEQ)]
    out += [(s, lax.rem(h + d, HEAD)) for d in range(1, HEAD)]
    out += [device(away(pos, axis, d), 1 - core) for axis in ("y", "z") for d in (1, 2, 3)]
    return out


class Ring:
    def __init__(self, pos, core, axis, buf, got, ssem, rsem):
        self.a0 = pos[axis]
        self.buf, self.got = buf, got
        up, down = device(away(pos, axis, 1), core), device(away(pos, axis, 3), core)
        far, nxt, prv = (lax.rem(self.a0 + d, 4) for d in (2, 1, 3))
        self.nxt, self.prv = nxt, prv
        route = ((far, 0, up), (far, 1, down), (nxt, 1, up), (prv, 0, down), (nxt, 0, up), (prv, 1, down))
        self.copies = [
            remote(buf.at[k, half], got.at[i], ssem.at[i], rsem.at[i], dev) for i, (k, half, dev) in enumerate(route)]

    def start(self):
        for c in self.copies[:4]:
            c.start()

    def relay(self):
        for i, k, half in ((0, self.nxt, 0), (1, self.prv, 1)):
            self.copies[i].wait_recv()
            total = self.buf[k, half].astype(f32) + self.got[i].astype(f32)
            self.buf[k, half] = total.astype(bf16)
            self.copies[4 + i].start()

    def finish(self):
        for i in (2, 3, 4, 5):
            self.copies[i].wait_recv()
        sums = []
        for half, i, j in ((0, 4, 3), (1, 2, 5)):
            sums.append(self.buf[self.a0, half].astype(f32) + self.got[i].astype(f32) + self.got[j].astype(f32))
        return sums

    def drain(self):
        for c in self.copies:
            c.wait_send()


class Direct:
    def __init__(self, pos, core, axis, buf, got, ssem, rsem):
        self.a0 = pos[axis]
        self.buf, self.got = buf, got
        self.copies = []
        for i, d in enumerate((2, 1, 3)):
            k = lax.rem(self.a0 + d, 4)
            for half in range(2):
                n = 2 * i + half
                self.copies.append(remote(buf.at[k, half], got.at[n], ssem.at[n], rsem.at[n], device(away(pos, axis, d), core)))

    def start(self):
        for c in self.copies:
            c.start()

    def relay(self):
        pass

    def finish(self):
        for c in self.copies:
            c.wait_recv()
        return [self.buf[self.a0, half].astype(f32) + self.got[half].astype(f32) + self.got[2 + half].astype(f32)
                + self.got[4 + half].astype(f32) for half in range(2)]

    def drain(self):
        for c in self.copies:
            c.wait_send()


def weight_part(p, left, left_r, right, right_r, core, g_s, out):
    own = pl.ds(pl.multiple_of(core * HALF + p * PART, PART), PART)
    theirs = pl.ds(p * PART, PART)

    @pl.loop(0, 4)
    def _(i):
        rows = pl.ds(pl.multiple_of(i * 384, 384), 384)
        g = dot_tn(left[:, rows], right[:, own]) + dot_tn(left_r[:, rows], right_r[:, theirs])
        if p == 0:
            for half in range(2):
                out[i, half] = g[half * 192:(half + 1) * 192].astype(bf16)
        else:
            g_s[i] = g

    def piece(y, z, x):
        return g_s[y, (z * 4 + x) * PIECE:(z * 4 + x + 1) * PIECE, :]

    if p > 0:
        for a in range(4):
            for b in range(4):
                rows = [piece(c, a, b) if p == 1 else piece(b, c, a) for c in range(4)]
                out[a, b // 2, (b % 2) * 96:(b % 2 + 1) * 96] = jnp.concatenate(rows, axis=0).astype(bf16)


def kernel(cnt, mod, lat, noise, times, inw, fc1_hbm, fc2_hbm, outw,
           mod_hbm, g_out, e_out,
           noisy_s, st_s, ni_s, ri_s, d_s, bo_s, ro_s, fin_s, pd_s, m_s, a1_s, a2_s,
           h, bg, bi, pg, mod_out, fc1, fc2,
           h_r, bg_r, bi_r, pg_r, g_s, s1, r1, s2, r2, q_s, u_s, l_r, e_s, ec_s, ec_r, e2_s, e2_r,
           load_sem, store_sem, pair_ss, pair_rs, ss1, rs1, ss2, rs2, ss3, rs3, ess, ers, fss, frs):
    pos, core = place()
    seq, head = lax.axis_index("seq"), lax.axis_index("head")
    barrier = pltpu.get_barrier_semaphore()
    met = peers(pos, core)
    for dev in met:
        pl.semaphore_signal(barrier, inc=1, device_id=dev, device_id_type=MESH)
    loads = [pltpu.make_async_copy(src, dst, load_sem.at[i]) for i, (src, dst) in enumerate(((fc1_hbm, fc1), (fc2_hbm, fc2)))]
    for c in loads:
        c.start()

    make_noisy(lat, noise, times, noisy_s)
    stream(noisy_s, inw, st_s)
    norm_in(mod, st_s, ni_s, ri_s, bi)
    pl.semaphore_wait(barrier, len(met))

    other = device(pos, 1 - core)
    theirs = pl.ds(pl.multiple_of((1 - core) * HALF, HALF), HALF)
    pair = [remote(src, dst, pair_ss.at[i], pair_rs.at[i], other) for i, (src, dst) in enumerate(
        ((bi, bi_r), (h, h_r), (bg.at[:, theirs], bg_r), (pg.at[:, theirs], pg_r)))]
    rings1 = [[Ring(pos, core, ORDER[p][0], s1.at[m, p], r1.at[m, p], ss1.at[m, p], rs1.at[m, p])
               for p in range(3)] for m in range(2)]
    rings2 = [[(Ring, Direct)[m](pos, core, ORDER[p][1], s2.at[m, p], r2.at[m, p], ss2.at[m, p], rs2.at[m, p])
               for p in range(3)] for m in range(2)]
    stores = [pltpu.make_async_copy(mod_out.at[:, b * W:(b + 1) * W], mod_hbm.at[:, b * W:(b + 1) * W], store_sem.at[b])
              for b in range(3)]

    def order(i):
        return lax.rem(i + 3 * (1 - core), 6)

    def pass1(m, left, left_r, right, right_r):
        for p in range(3):
            weight_part(p, left, left_r, right, right_r, core, g_s, s1.at[m, p])
            rings1[m][p].start()

    def pass2(m):
        for p in range(3):
            for hb, v in enumerate(rings1[m][p].finish()):
                v = v.astype(bf16)
                for b in range(2):
                    for hc in range(2):
                        at = (b * 2 + hc) * 48
                        s2[m, p, 2 * hb + b, hc] = v[at:at + 48]
            rings2[m][p].start()

    def pass3(m):
        for p in range(3):
            for hc, v in enumerate(rings2[m][p].finish()):
                for c in range(2):
                    q_s[p, 2 * hc + c, m * PIECE:(m + 1) * PIECE, :] = v[c * PIECE:(c + 1) * PIECE]

    def relays(rings):
        for r in rings:
            r.relay()

    pair[0].start()
    loads[0].wait()
    fc1_fwd(bi, fc1, h, d_s)
    pair[1].start()
    loads[1].wait()
    fc2_fwd(mod, h, fc2, st_s, bo_s)
    norm_out(st_s, ro_s, fin_s)
    predict(cnt, noise, fin_s, outw, pd_s, m_s)
    stream_grad(mod, pd_s, outw, st_s, ro_s, m_s, bo_s, bg, mod_out, order, (0, 3))
    pair[2].start()
    stream_grad(mod, pd_s, outw, st_s, ro_s, m_s, bo_s, bg, mod_out, order, (3, 6))
    stores[2].start()
    pair[1].wait_recv()
    pair[2].wait_recv()
    pass1(0, h, h_r, bg, bg_r)
    pre_grad(bg, fc2, d_s, pg, order, (0, 3))
    pair[3].start()
    relays(rings1[0])
    pre_grad(bg, fc2, d_s, pg, order, (3, 6))
    pair[0].wait_recv()
    pair[3].wait_recv()
    pass1(1, bi, bi_r, pg, pg_r)
    e_s[C:2 * C, 0:W] = dot(pd_s[...], fin_s[...])
    e_s[:, W:] = jnp.zeros((2 * C, 128), f32)
    a1_s[...] = jnp.zeros_like(a1_s)
    a2_s[...] = jnp.zeros_like(a2_s)
    block_grad(mod, pg, fc1, ni_s, st_s, a1_s, a2_s, mod_out, (0, 3))
    pass2(0)
    block_grad(mod, pg, fc1, ni_s, st_s, a1_s, a2_s, mod_out, (3, 6))
    stores[0].start()
    stores[1].start()
    relays(rings1[1])
    relays(rings2[0])
    input_grad(ri_s, ni_s, bo_s, st_s, a1_s, a2_s, fin_s)
    e_s[0:C, 0:W] = dot(noisy_s[...], fin_s[...])
    for k in range(SEQ):
        ec_s[k] = e_s[:, GROUP * k:GROUP * k + 128].astype(bf16)
    edge1 = [remote(ec_s.at[lax.rem(seq + d, SEQ)], ec_r.at[d - 1], ess.at[d - 1], ers.at[d - 1],
                    (lax.rem(seq + d, SEQ), head)) for d in range(1, SEQ)]
    for c in edge1:
        c.start()
    pass3(0)
    pass2(1)
    tot = ec_s[seq].astype(f32)
    for i, c in enumerate(edge1):
        c.wait_recv()
        tot = tot + ec_r[i].astype(f32)
    e2_s[...] = tot
    edge2 = [remote(e2_s, e2_r.at[d - 1], fss.at[d - 1], frs.at[d - 1], (seq, lax.rem(head + d, HEAD)))
             for d in range(1, HEAD)]
    for c in edge2:
        c.start()
    pass3(1)
    last = {}
    for p in range(3):
        axis = ORDER[p][2]
        for k in range(4):
            for c in range(2):
                v = [q_s[p, k, m * PIECE + c * 12:m * PIECE + c * 12 + 12] for m in range(2)]
                z = jnp.zeros((4, PART), f32)
                u_s[p, k, c] = jnp.concatenate([v[0], z, v[1], z], axis=0).astype(bf16)
        for rel in range(2):
            for d in range(1 - rel, 4):
                c = core if rel == 0 else 1 - core
                cp = remote(u_s.at[p, lax.rem(pos[axis] + d, 4), c], l_r.at[p, rel, d], ss3.at[p, rel, d],
                            rs3.at[p, rel, d], device(away(pos, axis, d), c))
                cp.start()
                last[p, rel, d] = cp
    for i, c in enumerate(edge2):
        c.wait_recv()
        tot = tot + e2_r[i]
    e_out[...] = pltpu.roll(tot * FACTOR, lax.rem(128 - 12 * head, 128), 1)
    mine = core * HALF
    for p in range(3):
        for rel in range(2):
            v = u_s[p, pos[ORDER[p][2]], core].astype(f32) if rel == 0 else None
            for d in range(1 - rel, 4):
                last[p, rel, d].wait_recv()
                t = l_r[p, rel, d].astype(f32)
                v = t if v is None else v + t
            v = v * FACTOR
            base = mine if rel == 0 else HALF - mine
            cols = pl.ds(pl.multiple_of(base + p * PART, PART), PART)
            g_out[:, cols] = v
    for m in range(2):
        for p in range(3):
            rings1[m][p].drain()
            rings2[m][p].drain()
    for c in pair + edge1 + edge2 + list(last.values()):
        c.wait_send()
    for c in stores:
        c.wait()


def fused_call(mod, lat, noise, times, cnt, inw, fc1, fc2, outw):
    v = pl.BlockSpec(memory_space=pltpu.VMEM)
    hbm = pl.BlockSpec(memory_space=pl.ANY)
    O = jax.ShapeDtypeStruct
    V = pltpu.VMEM
    D = pltpu.SemaphoreType.DMA
    big = V((R, W), bf16)
    half = V((R, HALF), bf16)
    return pl.pallas_call(
        kernel,
        out_shape=[O((ROWS, 3 * W), f32), O((32, W), f32), O((2 * C, 128), f32)],
        in_specs=[pl.BlockSpec(memory_space=pltpu.SMEM)] + [v] * 5 + [hbm, hbm, v],
        out_specs=[hbm, v, v],
        scratch_shapes=[
            V((C, R), bf16), V((R, W), f32), V((R, W), f32), V((R, 1), f32), V((R, W), f32), V((R, W), f32), V((R, 1), f32),
            big, V((C, R), bf16), V((R, 8), f32), V((R, 128), f32), V((R, 128), f32),
            big, big, big, big, V((ROWS, 3 * W), f32), V((W, W), bf16), V((W, W), bf16),
            big, half, big, half, V((4, 384, PART), f32),
            V((2, 3, 4, 2, 192, PART), bf16), V((2, 3, 6, 192, PART), bf16),
            V((2, 3, 4, 2, 48, PART), bf16), V((2, 3, 6, 48, PART), bf16),
            V((3, 4, 48, PART), f32), V((3, 4, 2, 32, PART), bf16), V((3, 2, 4, 32, PART), bf16),
            V((2 * C, W + 128), f32), V((SEQ, 2 * C, 128), bf16), V((SEQ - 1, 2 * C, 128), bf16),
            V((2 * C, 128), f32), V((HEAD - 1, 2 * C, 128), f32),
            D((2,)), D((3,)), D((4,)), D((4,)), D((2, 3, 6)), D((2, 3, 6)), D((2, 3, 6)), D((2, 3, 6)),
            D((3, 2, 4)), D((3, 2, 4)), D((SEQ - 1,)), D((SEQ - 1,)), D((HEAD - 1,)), D((HEAD - 1,)),
        ],
        compiler_params=pltpu.CompilerParams(
            collective_id=0, has_side_effects=True, vmem_limit_bytes=60 * 1024 * 1024),
        cost_estimate=pl.CostEstimate(flops=12 * R * W * W, bytes_accessed=20_000_000, transcendentals=R * W),
    )(cnt, mod, lat.T, noise.T, times.T, inw, fc1, fc2, outw)


def split_kernel(mod_hbm, g, e, mod_out, fc1_out, fc2_out, in_out, out_out, sem):
    c = pltpu.make_async_copy(mod_hbm, mod_out, sem)
    c.start()
    fc2_out[...] = g[0:12]
    fc1_out[...] = g[16:28]
    in_out[...] = e[0:C, 0:12]
    out_out[...] = e[C:2 * C, 0:12]
    c.wait()


def split_call(mod_grad, g, e):
    v = pl.BlockSpec(memory_space=pltpu.VMEM)
    hbm = pl.BlockSpec(memory_space=pl.ANY)
    O = jax.ShapeDtypeStruct
    return pl.pallas_call(
        split_kernel,
        out_shape=[O((ROWS, 3 * W), f32), O((12, W), f32), O((12, W), f32), O((C, 12), f32), O((C, 12), f32)],
        in_specs=[hbm, v, v],
        out_specs=[hbm, v, v, v, v],
        scratch_shapes=[pltpu.SemaphoreType.DMA],
    )(mod_grad, g, e)


def body(modulation, latents, noise, times, image_rows, in_weight, fc1_weight, fc2_weight, out_weight):
    mod_grad, g, e = fused_call(
        modulation, latents, noise, times, image_rows, in_weight, fc1_weight, fc2_weight, out_weight)
    return tuple(split_call(mod_grad, g, e))


def solution(mesh):
    rows = P(("seq", "head"), None)
    cols = P(None, ("seq", "head"))
    return jax.shard_map(
        body, mesh=mesh, in_specs=(rows, rows, rows, rows, P(("seq", "head")), P(), P(), P(), P()),
        out_specs=(rows, rows, rows, cols, cols), check_vma=False)
```

time: 103 us -> 141 us (1.37)
  Pallas kernels: 91.9 us -> 140 us
  local copies, waits for them, and re-layouts: 9.89 us -> 0 us
    pallas_call x2, Pallas kernels: 91.9 us -> 140 us  [the longest x1 74.2 us: split_call(): pl.pallas_call(split_kernel, out_shape=[O((ROWS, 3 * W), f32), O((12, W),...]
    unnamed x7 -> x0, local copies, waits for them, and re-layouts: 9.89 us -> none
where the time goes in v2:
time: 141 us
  Pallas kernels  140 us (99%)
    pallas_call x1, Pallas kernels, split_call(): pl.pallas_call(split_kernel, out_shape=[O((ROWS, 3 * W), f32), O((12, W),...  74.2 us
    pallas_call x1, Pallas kernels, fused_call(): pl.pallas_call(kernel, out_shape=[O((ROWS, 3 * W), f32), O((32, W), f32),...  65.8 us

profile of v2, /device:TPU:1, one launch (start us, length us, event | category | flops | bytes accessed | tf_op | source)
XLA Modules:
  0.0 141.3 jit_solution(12102132622846655168)
XLA Ops:
  1.3 65.8 %shard_map.128 = (f32[128,4608]{1,0:T(8,128)}, f32[32,1536]{1,0:T(8,128)}, f32[32,128]{1,0:T(8,128)}) custom-call(s32[1]{0:T(128)S(6)} %copy.14.cnt, bf16[128,4608]{1,0:T(8,128)(2,1)} %mod.1, bf16[16,128]{1,0:T(8,128)(2,1)} %bitcast.4, bf16[64,128]{1,0:T(8,128)(2,1)} %bitcast.3, bf16[4,128]{1,0:T(4,128)(2,1)} %bitcast.5, bf16[16,1536]{1,0:T(8,128)(2,1)} %inw.1, ...), custom_call_target="tpu_custom_call" | custom-call | flops 14495514624 | bytes 20000000 | tf_op jit(solution)/shard_map/pallas_call | solution.py:457
  67.1 74.2 %shard_map.129 = (f32[128,4608]{1,0:T(8,128)}, f32[12,1536]{1,0:T(8,128)}, f32[12,1536]{1,0:T(8,128)}, f32[16,12]{1,0:T(8,128)}, f32[16,12]{1,0:T(8,128)}) custom-call(f32[128,4608]{1,0:T(8,128)} %get-tuple-element.8.mod_hbm, f32[32,1536]{1,0:T(8,128)} %get-tuple-element.9.g, f32[32,128]{1,0:T(8,128)} %get-tuple-element.10.e), custom_call_target="tpu_custom_call" | custom-call | tf_op jit(solution)/shard_map/pallas_call | solution.py:495

commit v3 on v2

v3 whole, which is shorter than its diff:
```python
import jax
import jax.numpy as jnp
from jax import lax
from jax.experimental import pallas as pl
from jax.experimental.pallas import tpu as pltpu
from jax.sharding import PartitionSpec as P

f32, bf16 = jnp.float32, jnp.bfloat16
EPS = 1e-6
W, C, DRAWS, ROWS, NB = 1536, 16, 4, 128, 256
R = DRAWS * ROWS
NT = (((1,), (1,)), ((), ()))
TN = (((0,), (0,)), ((), ()))


def dot(a, b):
    return jnp.dot(a, b, preferred_element_type=f32)


def dot_nt(a, b):
    return lax.dot_general(a, b, NT, preferred_element_type=f32)


def dot_tn(a, b):
    return lax.dot_general(a, b, TN, preferred_element_type=f32)


def columns(j, base=0):
    if isinstance(j, int):
        return slice(base + j * NB, base + (j + 1) * NB)
    return pl.ds(pl.multiple_of(base + j * NB, NB), NB)


def draw(k):
    return slice(k * ROWS, (k + 1) * ROWS)


def make_noisy(lat, noise, times, noisy_s):
    ang = (0.5 * jnp.pi) * times[...].astype(f32)
    cosv, sinv = jnp.cos(ang), jnp.sin(ang)
    latv = lat[...].astype(f32)
    for k in range(DRAWS):
        nz = noise[C * k:C * (k + 1), :].astype(f32)
        noisy_s[:, draw(k)] = (cosv[k:k + 1, :] * latv + sinv[k:k + 1, :] * nz).astype(bf16)


def stream(noisy_s, inw, st_s):
    for j in range(W // NB):
        st_s[:, columns(j)] = dot_tn(noisy_s[...], inw[:, columns(j)])


def norm_in(mod, st_s, ni_s, ri_s, bi_s):
    for t0 in range(0, ROWS, 16):
        t = slice(t0, t0 + 16)
        for k in range(DRAWS):
            r = slice(k * ROWS + t0, k * ROWS + t0 + 16)
            x = st_s[r, :]
            c = x - jnp.mean(x, axis=-1, keepdims=True)
            rs = lax.rsqrt(jnp.mean(c * c, axis=-1, keepdims=True) + EPS)
            n = c * rs
            ni_s[r, :] = n
            ri_s[r, :] = rs
            bi_s[r, :] = (n * (1.0 + mod[t, W:2 * W].astype(f32)) + mod[t, 0:W].astype(f32)).astype(bf16)


def fc1_fwd(bi_s, fc1, h_s, d_s):
    for j in range(W // NB):
        hp = dot(bi_s[0:R, :], fc1[:, columns(j)])
        sg = jax.nn.sigmoid(hp)
        h_s[0:R, columns(j)] = (hp * sg).astype(bf16)
        d_s[:, columns(j)] = sg * (1.0 + hp * (1.0 - sg))


def fc2_fwd(mod, h_s, fc2, st_s, bo_s):
    for j in range(W // NB):
        bo = dot(h_s[0:R, :], fc2[:, columns(j)])
        bo_s[:, columns(j)] = bo
        gate = mod[:, columns(j, 2 * W)].astype(f32)
        for k in range(DRAWS):
            st_s[draw(k), columns(j)] = st_s[draw(k), columns(j)] + gate * bo[draw(k)]


def norm_out(st_s, ro_s, fin_s):
    for i in range(R // 32):
        r = slice(i * 32, (i + 1) * 32)
        x = st_s[r, :]
        c = x - jnp.mean(x, axis=-1, keepdims=True)
        rs = lax.rsqrt(jnp.mean(c * c, axis=-1, keepdims=True) + EPS)
        n = c * rs
        st_s[r, :] = n
        ro_s[r, :] = rs
        fin_s[r, :] = n.astype(bf16)


def predict(cnt, noise, fin_s, outw, pd_s, m_s):
    pred = dot_nt(outw[...], fin_s[...])
    ows = jnp.sum(outw[...].astype(f32), axis=-1, keepdims=True) * (1.0 / W)
    live = (lax.broadcasted_iota(jnp.int32, (1, ROWS), 1) < cnt[0]).astype(f32)
    for k in range(DRAWS):
        p = pred[:, draw(k)]
        pd = (2.0 * (p - noise[C * k:C * (k + 1), :].astype(f32)) * live).astype(bf16)
        pd_s[:, draw(k)] = pd
        pf = pd.astype(f32)
        m1 = jnp.sum(pf * ows, axis=0, keepdims=True)
        m2 = jnp.sum(pf * p, axis=0, keepdims=True) * (1.0 / W)
        m = jnp.concatenate([m1, m2, jnp.zeros((6, ROWS), f32)], axis=0)
        m_s[draw(k), :] = m.T


def stream_grad(j, own, mod, pd_s, outw, st_s, ro_s, m_s, bo_s, bg_s, bgx_s, mod_out):
    fg = dot_tn(pd_s[...], outw[:, columns(j)])
    gate = mod[:, columns(j, 2 * W)].astype(f32)
    acc = None
    for k in range(DRAWS):
        r = draw(k)
        sg = ro_s[r, :] * (fg[r] - m_s[r, 0:1] - st_s[r, columns(j)] * m_s[r, 1:2])
        bg = (sg * gate).astype(bf16)
        bg_s[r, columns(j)] = bg
        if own is not None:
            bgx_s[r, columns(own)] = bg
        t = sg * bo_s[r, columns(j)]
        bo_s[r, columns(j)] = sg
        acc = t if acc is None else acc + t
    mod_out[:, columns(j, 2 * W)] = acc


def pre_grad(j, own, bg_s, fc2, d_s, pg_s, pgx_s):
    ag = dot_nt(bg_s[...], fc2[columns(j), :])
    pg = (ag * d_s[:, columns(j)]).astype(bf16)
    pg_s[:, columns(j)] = pg
    if own is not None:
        pgx_s[0:R, columns(own)] = pg


def block_grad(j, mod, pg_s, fc1, ni_s, blk_s, a1_s, a2_s, mod_out):
    blk = dot_nt(pg_s[...], fc1[columns(j), :])
    sp = 1.0 + mod[:, columns(j, W)].astype(f32)
    s0 = s1 = None
    for k in range(DRAWS):
        r = draw(k)
        n = ni_s[r, columns(j)]
        b = blk[r]
        bn = b * n
        g = b * sp
        blk_s[r, columns(j)] = g
        gn = g * n
        t1, t2 = g[:, :128] + g[:, 128:], gn[:, :128] + gn[:, 128:]
        a1_s[r, :] = t1 if j == 0 else a1_s[r, :] + t1
        a2_s[r, :] = t2 if j == 0 else a2_s[r, :] + t2
        s0 = b if s0 is None else s0 + b
        s1 = bn if s1 is None else s1 + bn
    mod_out[:, columns(j)] = s0
    mod_out[:, columns(j, W)] = s1


def input_grad(ri_s, ni_s, sg_s, blk_s, a1_s, a2_s, ib_s):
    for i in range(R // 32):
        r = slice(i * 32, (i + 1) * 32)
        m1 = jnp.sum(a1_s[r, :], axis=-1, keepdims=True) * (1.0 / W)
        m2 = jnp.sum(a2_s[r, :], axis=-1, keepdims=True) * (1.0 / W)
        v = sg_s[r, :] + ri_s[r, :] * (blk_s[r, :] - m1 - ni_s[r, :] * m2)
        ib_s[r, :] = v.astype(bf16)


MESH = pl.DeviceIdType.MESH
ORDER = (("y", "x", "z"), ("z", "y", "x"), ("x", "z", "y"))
HALF, PART, PIECE = W // 2, W // 6, 24
FACTOR = (ROWS * 128 // 2) ** -0.5
SEQ, HEAD, SPLIT = 16, 8, 4
GROUP = W // SEQ


def place():
    s, h = lax.axis_index("seq"), lax.axis_index("head")
    return {"y": lax.div(s, 4), "z": lax.rem(s, 4), "x": lax.div(h, 2)}, lax.rem(h, 2)


def away(pos, axis, d):
    out = dict(pos)
    out[axis] = lax.rem(pos[axis] + d, 4)
    return out


def device(pos, core):
    return (pos["y"] * 4 + pos["z"], pos["x"] * 2 + core)


def remote(src, dst, ssem, rsem, dev):
    return pltpu.make_async_remote_copy(
        src_ref=src, dst_ref=dst, send_sem=ssem, recv_sem=rsem, device_id=dev, device_id_type=MESH)


def peers(pos, core):
    s, h = lax.axis_index("seq"), lax.axis_index("head")
    out = [(lax.rem(s + d, SEQ), h) for d in range(1, SEQ)]
    out += [(s, lax.rem(h + d, HEAD)) for d in range(1, HEAD)]
    out += [device(away(pos, axis, d), 1 - core) for axis in ("y", "z") for d in (1, 2, 3)]
    return out


class Ring:
    def __init__(self, pos, core, axis, buf, got, ssem, rsem):
        self.a0 = pos[axis]
        self.buf, self.got = buf, got
        up, down = device(away(pos, axis, 1), core), device(away(pos, axis, 3), core)
        far, nxt, prv = (lax.rem(self.a0 + d, 4) for d in (2, 1, 3))
        self.nxt, self.prv = nxt, prv
        route = ((far, 0, up), (far, 1, down), (nxt, 1, up), (prv, 0, down), (nxt, 0, up), (prv, 1, down))
        self.copies = [
            remote(buf.at[k, half], got.at[i], ssem.at[i], rsem.at[i], dev) for i, (k, half, dev) in enumerate(route)]

    def start(self):
        for c in self.copies[:4]:
            c.start()

    def relay(self):
        for i, k, half in ((0, self.nxt, 0), (1, self.prv, 1)):
            self.copies[i].wait_recv()
            total = self.buf[k, half].astype(f32) + self.got[i].astype(f32)
            self.buf[k, half] = total.astype(bf16)
            self.copies[4 + i].start()

    def finish(self):
        for i in (2, 3, 4, 5):
            self.copies[i].wait_recv()
        sums = []
        for half, i, j in ((0, 4, 3), (1, 2, 5)):
            sums.append(self.buf[self.a0, half].astype(f32) + self.got[i].astype(f32) + self.got[j].astype(f32))
        return sums

    def drain(self):
        for c in self.copies:
            c.wait_send()


class Direct:
    def __init__(self, pos, core, axis, buf, got, ssem, rsem):
        self.a0 = pos[axis]
        self.buf, self.got = buf, got
        self.copies = []
        for i, d in enumerate((2, 1, 3)):
            k = lax.rem(self.a0 + d, 4)
            for half in range(2):
                n = 2 * i + half
                self.copies.append(remote(buf.at[k, half], got.at[n], ssem.at[n], rsem.at[n], device(away(pos, axis, d), core)))

    def start(self):
        for c in self.copies:
            c.start()

    def relay(self):
        pass

    def finish(self):
        for c in self.copies:
            c.wait_recv()
        return [self.buf[self.a0, half].astype(f32) + self.got[half].astype(f32) + self.got[2 + half].astype(f32)
                + self.got[4 + half].astype(f32) for half in range(2)]

    def drain(self):
        for c in self.copies:
            c.wait_send()


def weight_part(p, left, right, out):
    prev = None
    for y in range(4):
        g = dot_tn(left[:, y * 384:(y + 1) * 384], right[:, p * PART:(p + 1) * PART])
        if p == 0:
            for x in range(4):
                v = jnp.concatenate([g[(z * 4 + x) * PIECE:(z * 4 + x + 1) * PIECE] for z in range(4)], axis=0)
                out[y, x // 2, (x % 2) * 96:(x % 2 + 1) * 96] = v.astype(bf16)
        elif p == 1:
            for z in range(4):
                out[z, y // 2, (y % 2) * 96:(y % 2 + 1) * 96] = g[z * 96:(z + 1) * 96].astype(bf16)
        elif y % 2 == 1:
            for z in range(4):
                for x in range(4):
                    at = (z * 4 + x) * PIECE
                    v = jnp.concatenate([prev[at:at + PIECE], g[at:at + PIECE]], axis=0)
                    to = (z % 2) * 96 + (y // 2) * 48
                    out[x, z // 2, to:to + 48] = v.astype(bf16)
        prev = g


def kernel(cnt, mod_in, lat, noise, times, inw, fc1_hbm, fc2_hbm, outw,
           mod_hbm, g_out, e_out,
           mod, noisy_s, st_s, ni_s, ri_s, d_s, bo_s, ro_s, fin_s, pd_s, m_s, a1_s, a2_s,
           hx, bix, bg, bgx, pg, pgx, mod_out, fc1, fc2,
           s1, r1, s2, r2, q_s, u_s, l_r, e_s, ec_s, ec_r, e2_s, e2_r,
           load_sem, store_sem, pair_ss, pair_rs, ss1, rs1, ss2, rs2, ss3, rs3, ess, ers, fss, frs):
    pos, core = place()
    seq, head = lax.axis_index("seq"), lax.axis_index("head")
    barrier = pltpu.get_barrier_semaphore()
    loads = [pltpu.make_async_copy(src, dst, load_sem.at[i])
             for i, (src, dst) in enumerate(((mod_in, mod), (fc1_hbm, fc1), (fc2_hbm, fc2)))]
    for c in loads:
        c.start()
    met = peers(pos, core)
    for dev in met:
        pl.semaphore_signal(barrier, inc=1, device_id=dev, device_id_type=MESH)

    make_noisy(lat, noise, times, noisy_s)
    stream(noisy_s, inw, st_s)
    loads[0].wait()
    norm_in(mod, st_s, ni_s, ri_s, bix)
    pl.semaphore_wait(barrier, len(met))

    other = device(pos, 1 - core)
    mine, theirs = core * 3, (1 - core) * 3
    low, high = pl.ds(0, R), pl.ds(R, R)
    pair = {}

    def to_pair(name, n, src, dst):
        pair[name] = remote(src, dst, pair_ss.at[n], pair_rs.at[n], other)
        pair[name].start()

    rings1 = [[Ring(pos, core, ORDER[p][0], s1.at[m, p], r1.at[m, p], ss1.at[m, p], rs1.at[m, p])
               for p in range(3)] for m in range(2)]
    rings2 = [[(Ring, Direct)[m](pos, core, ORDER[p][1], s2.at[m, p], r2.at[m, p], ss2.at[m, p], rs2.at[m, p])
               for p in range(3)] for m in range(2)]
    stores = [pltpu.make_async_copy(mod_out.at[:, b * W:(b + 1) * W], mod_hbm.at[:, b * W:(b + 1) * W], store_sem.at[b])
              for b in range(3)]

    def pass1(m, left, right, name):
        for p in range(3):
            pair[name, p].wait_recv()
            weight_part(p, left, right, s1.at[m, p])
            rings1[m][p].start()

    def pass2(m, p):
        for hb, v in enumerate(rings1[m][p].finish()):
            v = v.astype(bf16)
            for b in range(2):
                for hc in range(2):
                    at = (b * 2 + hc) * 48
                    s2[m, p, 2 * hb + b, hc] = v[at:at + 48]
        rings2[m][p].start()

    def pass3(m, p):
        for hc, v in enumerate(rings2[m][p].finish()):
            for c in range(2):
                q_s[p, 2 * hc + c, m * PIECE:(m + 1) * PIECE, :] = v[c * PIECE:(c + 1) * PIECE]

    to_pair("bi", 0, bix.at[low], bix.at[high])
    loads[1].wait()
    fc1_fwd(bix, fc1, hx, d_s)
    to_pair("h", 1, hx.at[low], hx.at[high])
    loads[2].wait()
    fc2_fwd(mod, hx, fc2, st_s, bo_s)
    norm_out(st_s, ro_s, fin_s)
    predict(cnt, noise, fin_s, outw, pd_s, m_s)
    for i in range(6):
        j = (theirs if i < 3 else mine) + i % 3
        stream_grad(j, i - 3 if i >= 3 else None, mod, pd_s, outw, st_s, ro_s, m_s, bo_s, bg, bgx, mod_out)
        if i < 3:
            to_pair(("bg", i), 2 + i, bg.at[:, columns(j)], bgx.at[high, columns(i)])
    stores[2].start()
    pair["h"].wait_recv()
    pass1(0, hx, bgx, "bg")
    for i in range(6):
        j = (theirs if i < 3 else mine) + i % 3
        pre_grad(j, i - 3 if i >= 3 else None, bg, fc2, d_s, pg, pgx)
        if i < 3:
            to_pair(("pg", i), 5 + i, pg.at[:, columns(j)], pgx.at[high, columns(i)])
        else:
            rings1[0][i - 3].relay()
    pair["bi"].wait_recv()
    pass1(1, bix, pgx, "pg")
    e_s[C:2 * C, 0:W] = dot(pd_s[...], fin_s[...])
    e_s[:, W:] = jnp.zeros((2 * C, 128), f32)
    for j in range(6):
        block_grad(j, mod, pg, fc1, ni_s, st_s, a1_s, a2_s, mod_out)
        if j >= 3:
            pass2(0, j - 3)
    stores[0].start()
    stores[1].start()
    for p in range(3):
        rings1[1][p].relay()
    for p in range(3):
        rings2[0][p].relay()
    input_grad(ri_s, ni_s, bo_s, st_s, a1_s, a2_s, fin_s)
    e_s[0:C, 0:W] = dot(noisy_s[...], fin_s[...])
    for k in range(SEQ):
        ec_s[k] = e_s[:, GROUP * k:GROUP * k + 128].astype(bf16)
    edge1 = [remote(ec_s.at[lax.rem(seq + d, SEQ)], ec_r.at[d - 1], ess.at[d - 1], ers.at[d - 1],
                    (lax.rem(seq + d, SEQ), head)) for d in range(1, SEQ)]
    for c in edge1:
        c.start()
    for p in range(3):
        pass3(0, p)
    for p in range(3):
        pass2(1, p)
    tot = ec_s[seq].astype(f32)
    for i, c in enumerate(edge1):
        c.wait_recv()
        tot = tot + ec_r[i].astype(f32)
    e2_s[...] = tot
    edge2 = [remote(e2_s, e2_r.at[d - 1], fss.at[d - 1], frs.at[d - 1], (seq, lax.rem(head + d, HEAD)))
             for d in range(1, HEAD)]
    for c in edge2:
        c.start()
    last = {}
    for p in range(3):
        pass3(1, p)
        axis = ORDER[p][2]
        for k in range(4):
            for c in range(2):
                v = [q_s[p, k, m * PIECE + c * 12:m * PIECE + c * 12 + 12] for m in range(2)]
                z = jnp.zeros((4, PART), f32)
                u_s[p, k, c] = jnp.concatenate([v[0], z, v[1], z], axis=0).astype(bf16)
        for rel in range(2):
            for d in range(1 - rel, 4):
                c = core if rel == 0 else 1 - core
                cp = remote(u_s.at[p, lax.rem(pos[axis] + d, 4), c], l_r.at[p, rel, d], ss3.at[p, rel, d],
                            rs3.at[p, rel, d], device(away(pos, axis, d), c))
                cp.start()
                last[p, rel, d] = cp
    for i, c in enumerate(edge2):
        c.wait_recv()
        tot = tot + e2_r[i]
    e_out[...] = pltpu.roll(tot * FACTOR, lax.rem(128 - 12 * head, 128), 1)
    for p in range(3):
        for rel in range(2):
            v = u_s[p, pos[ORDER[p][2]], core].astype(f32) if rel == 0 else None
            for d in range(1 - rel, 4):
                last[p, rel, d].wait_recv()
                t = l_r[p, rel, d].astype(f32)
                v = t if v is None else v + t
            g_out[:, columns((mine if rel == 0 else theirs) + p)] = v * FACTOR
    for m in range(2):
        for p in range(3):
            rings1[m][p].drain()
            rings2[m][p].drain()
    for c in list(pair.values()) + edge1 + edge2 + list(last.values()):
        c.wait_send()
    for c in stores:
        c.wait()


def fused_call(mod, lat, noise, times, cnt, inw, fc1, fc2, outw):
    v = pl.BlockSpec(memory_space=pltpu.VMEM)
    hbm = pl.BlockSpec(memory_space=pl.ANY)
    O = jax.ShapeDtypeStruct
    V = pltpu.VMEM
    D = pltpu.SemaphoreType.DMA
    big = V((R, W), bf16)
    two = V((2 * R, W), bf16)
    half = V((2 * R, HALF), bf16)
    return pl.pallas_call(
        kernel,
        out_shape=[O((ROWS, 3 * W), f32), O((32, W), f32), O((2 * C, 128), f32)],
        in_specs=[pl.BlockSpec(memory_space=pltpu.SMEM), hbm, v, v, v, v, hbm, hbm, v],
        out_specs=[hbm, v, v],
        scratch_shapes=[
            V((ROWS, 3 * W), bf16), V((C, R), bf16), V((R, W), f32), V((R, W), f32), V((R, 1), f32), V((R, W), f32),
            V((R, W), f32), V((R, 1), f32), big, V((C, R), bf16), V((R, 8), f32), V((R, 128), f32), V((R, 128), f32),
            two, two, big, half, big, half, V((ROWS, 3 * W), f32), V((W, W), bf16), V((W, W), bf16),
            V((2, 3, 4, 2, 192, PART), bf16), V((2, 3, 6, 192, PART), bf16),
            V((2, 3, 4, 2, 48, PART), bf16), V((2, 3, 6, 48, PART), bf16),
            V((3, 4, 48, PART), f32), V((3, 4, 2, 32, PART), bf16), V((3, 2, 4, 32, PART), bf16),
            V((2 * C, W + 128), f32), V((SEQ, 2 * C, 128), bf16), V((SEQ - 1, 2 * C, 128), bf16),
            V((2 * C, 128), f32), V((HEAD - 1, 2 * C, 128), f32),
            D((3,)), D((3,)), D((8,)), D((8,)), D((2, 3, 6)), D((2, 3, 6)), D((2, 3, 6)), D((2, 3, 6)),
            D((3, 2, 4)), D((3, 2, 4)), D((SEQ - 1,)), D((SEQ - 1,)), D((HEAD - 1,)), D((HEAD - 1,)),
        ],
        compiler_params=pltpu.CompilerParams(
            collective_id=0, has_side_effects=True, vmem_limit_bytes=60 * 1024 * 1024),
        cost_estimate=pl.CostEstimate(flops=12 * R * W * W, bytes_accessed=20_000_000, transcendentals=R * W),
    )(cnt, mod, lat.T, noise.T, times.T, inw, fc1, fc2, outw)


def split_kernel(mod_hbm, g, e, mod_out, fc1_out, fc2_out, in_out, out_out, buf, in_sem, out_sem):
    n = ROWS // SPLIT
    parts = [pl.ds(i * n, n) for i in range(SPLIT)]
    into = [pltpu.make_async_copy(mod_hbm.at[r], buf.at[r], in_sem.at[i]) for i, r in enumerate(parts)]
    out = [pltpu.make_async_copy(buf.at[r], mod_out.at[r], out_sem.at[i]) for i, r in enumerate(parts)]
    for c in into:
        c.start()
    fc2_out[...] = g[0:12]
    fc1_out[...] = g[16:28]
    in_out[...] = e[0:C, 0:12]
    out_out[...] = e[C:2 * C, 0:12]
    for a, b in zip(into, out):
        a.wait()
        b.start()
    for c in out:
        c.wait()


def split_call(mod_grad, g, e):
    v = pl.BlockSpec(memory_space=pltpu.VMEM)
    hbm = pl.BlockSpec(memory_space=pl.ANY)
    O = jax.ShapeDtypeStruct
    return pl.pallas_call(
        split_kernel,
        out_shape=[O((ROWS, 3 * W), f32), O((12, W), f32), O((12, W), f32), O((C, 12), f32), O((C, 12), f32)],
        in_specs=[hbm, v, v],
        out_specs=[hbm, v, v, v, v],
        scratch_shapes=[pltpu.VMEM((ROWS, 3 * W), f32), pltpu.SemaphoreType.DMA((SPLIT,)), pltpu.SemaphoreType.DMA((SPLIT,))],
        compiler_params=pltpu.CompilerParams(vmem_limit_bytes=60 * 1024 * 1024),
    )(mod_grad, g, e)


def body(modulation, latents, noise, times, image_rows, in_weight, fc1_weight, fc2_weight, out_weight):
    mod_grad, g, e = fused_call(
        modulation, latents, noise, times, image_rows, in_weight, fc1_weight, fc2_weight, out_weight)
    return tuple(split_call(mod_grad, g, e))


def solution(mesh):
    rows = P(("seq", "head"), None)
    cols = P(None, ("seq", "head"))
    return jax.shard_map(
        body, mesh=mesh, in_specs=(rows, rows, rows, rows, P(("seq", "head")), P(), P(), P(), P()),
        out_specs=(rows, rows, rows, cols, cols), check_vma=False)
```

time: 141 us -> 61.4 us (0.44)
  Pallas kernels: 140 us -> 59.7 us
    pallas_call x1, Pallas kernels: 74.2 us -> 4.14 us  [split_call(): pl.pallas_call(split_kernel, out_shape=[O((ROWS, 3 * W), f32), O((12, W),...]
    pallas_call x1, Pallas kernels: 65.8 us -> 55.6 us  [fused_call(): pl.pallas_call(kernel, out_shape=[O((ROWS, 3 * W), f32), O((32, W), f32),...]
where the time goes in v3:
time: 61.4 us; the launch traced here: 61.1 us
  Pallas kernels  59.7 us (97%)
  between operations  1.45 us (2%)
    pallas_call x1, Pallas kernels, fused_call(): pl.pallas_call(kernel, out_shape=[O((ROWS, 3 * W), f32), O((32, W), f32),...  55.6 us
    pallas_call x1, Pallas kernels, split_call(): pl.pallas_call(split_kernel, out_shape=[O((ROWS, 3 * W), f32), O((12, W),...  4.14 us

profile of v3, /device:TPU:1, one launch (start us, length us, event | category | flops | bytes accessed | tf_op | source)
XLA Modules:
  0.0 61.1 jit_solution(14818721202476734802)
XLA Ops:
  1.3 55.6 %shard_map.128 = (f32[128,4608]{1,0:T(8,128)}, f32[32,1536]{1,0:T(8,128)}, f32[32,128]{1,0:T(8,128)}) custom-call(s32[1]{0:T(128)S(6)} %copy.14.cnt, bf16[128,4608]{1,0:T(8,128)(2,1)} %mod_in.1, bf16[16,128]{1,0:T(8,128)(2,1)} %bitcast.4, bf16[64,128]{1,0:T(8,128)(2,1)} %bitcast.3, bf16[4,128]{1,0:T(4,128)(2,1)} %bitcast.5, bf16[16,1536]{1,0:T(8,128)(2,1)} %inw.1, ...), custom_call_target="tpu_custom_call" | custom-call | flops 14495514624 | bytes 20000000 | tf_op jit(solution)/shard_map/pallas_call | solution.py:450
  56.8 4.1 %shard_map.129 = (f32[128,4608]{1,0:T(8,128)}, f32[12,1536]{1,0:T(8,128)}, f32[12,1536]{1,0:T(8,128)}, f32[16,12]{1,0:T(8,128)}, f32[16,12]{1,0:T(8,128)}) custom-call(f32[128,4608]{1,0:T(8,128)} %get-tuple-element.8.mod_hbm, f32[32,1536]{1,0:T(8,128)} %get-tuple-element.9.g, f32[32,128]{1,0:T(8,128)} %get-tuple-element.10.e), custom_call_target="tpu_custom_call" | custom-call | tf_op jit(solution)/shard_map/pallas_call | solution.py:495

commit v4 on v3

--- a/solution.py
+++ b/solution.py
@@ -80,9 +80,9 @@
             st_s[draw(k), columns(j)] = st_s[draw(k), columns(j)] + gate * bo[draw(k)]
 
 
-def norm_out(st_s, ro_s, fin_s):
-    for i in range(R // 32):
-        r = slice(i * 32, (i + 1) * 32)
+def norm_out(k, st_s, ro_s, fin_s):
+    for i in range(ROWS // 32):
+        r = slice(k * ROWS + i * 32, k * ROWS + (i + 1) * 32)
         x = st_s[r, :]
         c = x - jnp.mean(x, axis=-1, keepdims=True)
         rs = lax.rsqrt(jnp.mean(c * c, axis=-1, keepdims=True) + EPS)
@@ -92,36 +92,30 @@
         fin_s[r, :] = n.astype(bf16)
 
 
-def predict(cnt, noise, fin_s, outw, pd_s, m_s):
-    pred = dot_nt(outw[...], fin_s[...])
+def predict(k, cnt, noise, fin_s, outw, pd_s, m_s):
+    p = dot_nt(outw[...], fin_s[draw(k), :])
     ows = jnp.sum(outw[...].astype(f32), axis=-1, keepdims=True) * (1.0 / W)
     live = (lax.broadcasted_iota(jnp.int32, (1, ROWS), 1) < cnt[0]).astype(f32)
-    for k in range(DRAWS):
-        p = pred[:, draw(k)]
-        pd = (2.0 * (p - noise[C * k:C * (k + 1), :].astype(f32)) * live).astype(bf16)
-        pd_s[:, draw(k)] = pd
-        pf = pd.astype(f32)
-        m1 = jnp.sum(pf * ows, axis=0, keepdims=True)
-        m2 = jnp.sum(pf * p, axis=0, keepdims=True) * (1.0 / W)
-        m = jnp.concatenate([m1, m2, jnp.zeros((6, ROWS), f32)], axis=0)
-        m_s[draw(k), :] = m.T
-
-
-def stream_grad(j, own, mod, pd_s, outw, st_s, ro_s, m_s, bo_s, bg_s, bgx_s, mod_out):
+    pd = (2.0 * (p - noise[C * k:C * (k + 1), :].astype(f32)) * live).astype(bf16)
+    pd_s[:, draw(k)] = pd
+    pf = pd.astype(f32)
+    m1 = jnp.sum(pf * ows, axis=0, keepdims=True)
+    m2 = jnp.sum(pf * p, axis=0, keepdims=True) * (1.0 / W)
+    m = jnp.concatenate([m1, m2, jnp.zeros((6, ROWS), f32)], axis=0)
+    m_s[draw(k), :] = m.T
+
+
+def stream_grad(j, own, mod, pd_s, outw, st_s, ro_s, m_s, sg_s, bg_s, bgx_s):
     fg = dot_tn(pd_s[...], outw[:, columns(j)])
     gate = mod[:, columns(j, 2 * W)].astype(f32)
-    acc = None
     for k in range(DRAWS):
         r = draw(k)
         sg = ro_s[r, :] * (fg[r] - m_s[r, 0:1] - st_s[r, columns(j)] * m_s[r, 1:2])
         bg = (sg * gate).astype(bf16)
+        sg_s[r, columns(j)] = sg
         bg_s[r, columns(j)] = bg
         if own is not None:
             bgx_s[r, columns(own)] = bg
-        t = sg * bo_s[r, columns(j)]
-        bo_s[r, columns(j)] = sg
-        acc = t if acc is None else acc + t
-    mod_out[:, columns(j, 2 * W)] = acc
 
 
 def pre_grad(j, own, bg_s, fc2, d_s, pg_s, pgx_s):
@@ -132,10 +126,10 @@
         pgx_s[0:R, columns(own)] = pg
 
 
-def block_grad(j, mod, pg_s, fc1, ni_s, blk_s, a1_s, a2_s, mod_out):
+def block_grad(j, mod, pg_s, fc1, ni_s, sg_s, bo_s, blk_s, a1_s, a2_s, mod_out):
     blk = dot_nt(pg_s[...], fc1[columns(j), :])
     sp = 1.0 + mod[:, columns(j, W)].astype(f32)
-    s0 = s1 = None
+    s0 = s1 = s2 = None
     for k in range(DRAWS):
         r = draw(k)
         n = ni_s[r, columns(j)]
@@ -149,8 +143,11 @@
         a2_s[r, :] = t2 if j == 0 else a2_s[r, :] + t2
         s0 = b if s0 is None else s0 + b
         s1 = bn if s1 is None else s1 + bn
+        t = sg_s[r, columns(j)] * bo_s[r, columns(j)]
+        s2 = t if s2 is None else s2 + t
     mod_out[:, columns(j)] = s0
     mod_out[:, columns(j, W)] = s1
+    mod_out[:, columns(j, 2 * W)] = s2
 
 
 def input_grad(ri_s, ni_s, sg_s, blk_s, a1_s, a2_s, ib_s):
@@ -210,7 +207,15 @@
             remote(buf.at[k, half], got.at[i], ssem.at[i], rsem.at[i], dev) for i, (k, half, dev) in enumerate(route)]
 
     def start(self):
-        for c in self.copies[:4]:
+        self.start_far()
+        self.start_near()
+
+    def start_far(self):
+        for c in self.copies[:2]:
+            c.start()
+
+    def start_near(self):
+        for c in self.copies[2:4]:
             c.start()
 
     def relay(self):
@@ -262,39 +267,56 @@
             c.wait_send()
 
 
-def weight_part(p, left, right, out):
+def weight_own(left, right, acc):
+    for y in range(2):
+        acc[y] = dot_tn(left[0:R, y * 384:(y + 1) * 384], right[0:R, :])
+
+
+def weight_parts(left, right, acc, out):
     prev = None
     for y in range(4):
-        g = dot_tn(left[:, y * 384:(y + 1) * 384], right[:, p * PART:(p + 1) * PART])
-        if p == 0:
-            for x in range(4):
-                v = jnp.concatenate([g[(z * 4 + x) * PIECE:(z * 4 + x + 1) * PIECE] for z in range(4)], axis=0)
-                out[y, x // 2, (x % 2) * 96:(x % 2 + 1) * 96] = v.astype(bf16)
-        elif p == 1:
-            for z in range(4):
-                out[z, y // 2, (y % 2) * 96:(y % 2 + 1) * 96] = g[z * 96:(z + 1) * 96].astype(bf16)
-        elif y % 2 == 1:
+        rows = slice(y * 384, (y + 1) * 384)
+        if y < 2:
+            g = acc[y] + dot_tn(left[R:2 * R, rows], right[R:2 * R, :])
+        else:
+            g = dot_tn(left[:, rows], right[...])
+        g0, g1, g2 = (g[:, p * PART:(p + 1) * PART] for p in range(3))
+        for x in range(4):
+            v = jnp.concatenate([g0[(z * 4 + x) * PIECE:(z * 4 + x + 1) * PIECE] for z in range(4)], axis=0)
+            out[0, y, x // 2, (x % 2) * 96:(x % 2 + 1) * 96] = v.astype(bf16)
+        for z in range(4):
+            out[1, z, y // 2, (y % 2) * 96:(y % 2 + 1) * 96] = g1[z * 96:(z + 1) * 96].astype(bf16)
+        if y % 2 == 1:
             for z in range(4):
                 for x in range(4):
                     at = (z * 4 + x) * PIECE
-                    v = jnp.concatenate([prev[at:at + PIECE], g[at:at + PIECE]], axis=0)
+                    v = jnp.concatenate([prev[at:at + PIECE], g2[at:at + PIECE]], axis=0)
                     to = (z % 2) * 96 + (y // 2) * 48
-                    out[x, z // 2, to:to + 48] = v.astype(bf16)
-        prev = g
+                    out[2, x, z // 2, to:to + 48] = v.astype(bf16)
+        prev = g2
 
 
 def kernel(cnt, mod_in, lat, noise, times, inw, fc1_hbm, fc2_hbm, outw,
            mod_hbm, g_out, e_out,
-           mod, noisy_s, st_s, ni_s, ri_s, d_s, bo_s, ro_s, fin_s, pd_s, m_s, a1_s, a2_s,
+           mod, noisy_s, st_s, ni_s, ri_s, d_s, bo_s, sg_s, ro_s, fin_s, pd_s, m_s, a1_s, a2_s,
            hx, bix, bg, bgx, pg, pgx, mod_out, fc1, fc2,
-           s1, r1, s2, r2, q_s, u_s, l_r, e_s, ec_s, ec_r, e2_s, e2_r,
-           load_sem, store_sem, pair_ss, pair_rs, ss1, rs1, ss2, rs2, ss3, rs3, ess, ers, fss, frs):
+           acc, s1, r1, s2, r2, u_s, l_r, e_s, ec_s, ec_r, e2_s, e2_r, g_s, ee_s,
+           load_sem, store_sem, pair_ss, pair_rs, ss1, rs1, ss2, rs2, ss3, rs3, ess, ers, fss, frs, out_sem):
     pos, core = place()
     seq, head = lax.axis_index("seq"), lax.axis_index("head")
     barrier = pltpu.get_barrier_semaphore()
-    loads = [pltpu.make_async_copy(src, dst, load_sem.at[i])
-             for i, (src, dst) in enumerate(((mod_in, mod), (fc1_hbm, fc1), (fc2_hbm, fc2)))]
-    for c in loads:
+    def load(n, src, dst):
+        return [pltpu.make_async_copy(src.at[pl.ds(i * 384, 384)], dst.at[pl.ds(i * 384, 384)], load_sem.at[n, i])
+                for i in range(4)]
+
+    def wait(copies):
+        for c in copies:
+            c.wait()
+
+    mod_load = pltpu.make_async_copy(mod_in, mod, load_sem.at[2, 0])
+    mod_load.start()
+    fc1_load, fc2_load = load(0, fc1_hbm, fc1), load(1, fc2_hbm, fc2)
+    for c in fc1_load:
         c.start()
     met = peers(pos, core)
     for dev in met:
@@ -302,12 +324,13 @@
 
     make_noisy(lat, noise, times, noisy_s)
     stream(noisy_s, inw, st_s)
-    loads[0].wait()
+    mod_load.wait()
     norm_in(mod, st_s, ni_s, ri_s, bix)
     pl.semaphore_wait(barrier, len(met))
 
     other = device(pos, 1 - core)
     mine, theirs = core * 3, (1 - core) * 3
+    half_at = pl.ds(pl.multiple_of((1 - core) * HALF, HALF), HALF)
     low, high = pl.ds(0, R), pl.ds(R, R)
     pair = {}
 
@@ -317,16 +340,14 @@
 
     rings1 = [[Ring(pos, core, ORDER[p][0], s1.at[m, p], r1.at[m, p], ss1.at[m, p], rs1.at[m, p])
                for p in range(3)] for m in range(2)]
-    rings2 = [[(Ring, Direct)[m](pos, core, ORDER[p][1], s2.at[m, p], r2.at[m, p], ss2.at[m, p], rs2.at[m, p])
+    rings2 = [[Direct(pos, core, ORDER[p][1], s2.at[m, p], r2.at[m, p], ss2.at[m, p], rs2.at[m, p])
                for p in range(3)] for m in range(2)]
     stores = [pltpu.make_async_copy(mod_out.at[:, b * W:(b + 1) * W], mod_hbm.at[:, b * W:(b + 1) * W], store_sem.at[b])
               for b in range(3)]
 
-    def pass1(m, left, right, name):
+    def each(m, name):
         for p in range(3):
-            pair[name, p].wait_recv()
-            weight_part(p, left, right, s1.at[m, p])
-            rings1[m][p].start()
+            getattr(rings1[m][p], name)()
 
     def pass2(m, p):
         for hb, v in enumerate(rings1[m][p].finish()):
@@ -338,59 +359,94 @@
         rings2[m][p].start()
 
     def pass3(m, p):
+        z = jnp.zeros((4, PART), f32)
         for hc, v in enumerate(rings2[m][p].finish()):
-            for c in range(2):
-                q_s[p, 2 * hc + c, m * PIECE:(m + 1) * PIECE, :] = v[c * PIECE:(c + 1) * PIECE]
+            for k in range(2):
+                for c in range(2):
+                    at = k * PIECE + c * 12
+                    u_s[m, p, 2 * hc + k, c] = jnp.concatenate([v[at:at + 12], z], axis=0).astype(bf16)
+
+    def finish_part(m, p):
+        pass3(m, p)
+        axis = ORDER[p][2]
+        for rel in range(2):
+            for d in range(1 - rel, 4):
+                c = core if rel == 0 else 1 - core
+                cp = remote(u_s.at[m, p, lax.rem(pos[axis] + d, 4), c], l_r.at[m, p, rel, d], ss3.at[m, p, rel, d],
+                            rs3.at[m, p, rel, d], device(away(pos, axis, d), c))
+                cp.start()
+                last[m, p, rel, d] = cp
+
+    out_copies = [pltpu.make_async_copy(g_s.at[pl.ds(16 * m, 16)], g_out.at[pl.ds(16 * m, 16)], out_sem.at[m]) for m in range(2)]
+    out_copies.append(pltpu.make_async_copy(ee_s, e_out, out_sem.at[2]))
+
+    def take(m):
+        for p in range(3):
+            for rel in range(2):
+                v = u_s[m, p, pos[ORDER[p][2]], core].astype(f32) if rel == 0 else None
+                for d in range(1 - rel, 4):
+                    last[m, p, rel, d].wait_recv()
+                    t = l_r[m, p, rel, d].astype(f32)
+                    v = t if v is None else v + t
+                g_s[m * 16:(m + 1) * 16, columns((mine if rel == 0 else theirs) + p)] = v * FACTOR
+        out_copies[m].start()
 
     to_pair("bi", 0, bix.at[low], bix.at[high])
-    loads[1].wait()
+    wait(fc1_load)
+    for c in fc2_load:
+        c.start()
     fc1_fwd(bix, fc1, hx, d_s)
     to_pair("h", 1, hx.at[low], hx.at[high])
-    loads[2].wait()
+    wait(fc2_load)
     fc2_fwd(mod, hx, fc2, st_s, bo_s)
-    norm_out(st_s, ro_s, fin_s)
-    predict(cnt, noise, fin_s, outw, pd_s, m_s)
-    for i in range(6):
-        j = (theirs if i < 3 else mine) + i % 3
-        stream_grad(j, i - 3 if i >= 3 else None, mod, pd_s, outw, st_s, ro_s, m_s, bo_s, bg, bgx, mod_out)
-        if i < 3:
-            to_pair(("bg", i), 2 + i, bg.at[:, columns(j)], bgx.at[high, columns(i)])
-    stores[2].start()
+    for k in range(DRAWS):
+        norm_out(k, st_s, ro_s, fin_s)
+        predict(k, cnt, noise, fin_s, outw, pd_s, m_s)
+    for i in range(3):
+        stream_grad(theirs + i, None, mod, pd_s, outw, st_s, ro_s, m_s, sg_s, bg, bgx)
+    to_pair("bg", 2, bg.at[:, half_at], bgx.at[high])
+    for i in range(3):
+        stream_grad(mine + i, i, mod, pd_s, outw, st_s, ro_s, m_s, sg_s, bg, bgx)
+    weight_own(hx, bgx, acc)
     pair["h"].wait_recv()
-    pass1(0, hx, bgx, "bg")
-    for i in range(6):
-        j = (theirs if i < 3 else mine) + i % 3
-        pre_grad(j, i - 3 if i >= 3 else None, bg, fc2, d_s, pg, pgx)
-        if i < 3:
-            to_pair(("pg", i), 5 + i, pg.at[:, columns(j)], pgx.at[high, columns(i)])
-        else:
-            rings1[0][i - 3].relay()
+    pair["bg"].wait_recv()
+    weight_parts(hx, bgx, acc, s1.at[0])
+    each(0, "start_far")
+    each(0, "start_near")
+    for i in range(3):
+        pre_grad(theirs + i, None, bg, fc2, d_s, pg, pgx)
+    to_pair("pg", 3, pg.at[:, half_at], pgx.at[high])
+    for i in range(3):
+        pre_grad(mine + i, i, bg, fc2, d_s, pg, pgx)
+    weight_own(bix, pgx, acc)
+    each(0, "relay")
     pair["bi"].wait_recv()
-    pass1(1, bix, pgx, "pg")
+    pair["pg"].wait_recv()
+    weight_parts(bix, pgx, acc, s1.at[1])
+    each(1, "start_far")
+    each(1, "start_near")
     e_s[C:2 * C, 0:W] = dot(pd_s[...], fin_s[...])
     e_s[:, W:] = jnp.zeros((2 * C, 128), f32)
     for j in range(6):
-        block_grad(j, mod, pg, fc1, ni_s, st_s, a1_s, a2_s, mod_out)
-        if j >= 3:
-            pass2(0, j - 3)
-    stores[0].start()
-    stores[1].start()
+        block_grad(j, mod, pg, fc1, ni_s, sg_s, bo_s, st_s, a1_s, a2_s, mod_out)
+    for c in stores:
+        c.start()
     for p in range(3):
-        rings1[1][p].relay()
-    for p in range(3):
-        rings2[0][p].relay()
-    input_grad(ri_s, ni_s, bo_s, st_s, a1_s, a2_s, fin_s)
+        pass2(0, p)
+    input_grad(ri_s, ni_s, sg_s, st_s, a1_s, a2_s, fin_s)
     e_s[0:C, 0:W] = dot(noisy_s[...], fin_s[...])
     for k in range(SEQ):
         ec_s[k] = e_s[:, GROUP * k:GROUP * k + 128].astype(bf16)
+    each(1, "relay")
     edge1 = [remote(ec_s.at[lax.rem(seq + d, SEQ)], ec_r.at[d - 1], ess.at[d - 1], ers.at[d - 1],
                     (lax.rem(seq + d, SEQ), head)) for d in range(1, SEQ)]
     for c in edge1:
         c.start()
     for p in range(3):
-        pass3(0, p)
+        pass2(1, p)
+    last = {}
     for p in range(3):
-        pass2(1, p)
+        finish_part(0, p)
     tot = ec_s[seq].astype(f32)
     for i, c in enumerate(edge1):
         c.wait_recv()
@@ -400,41 +456,22 @@
              for d in range(1, HEAD)]
     for c in edge2:
         c.start()
-    last = {}
     for p in range(3):
-        pass3(1, p)
-        axis = ORDER[p][2]
-        for k in range(4):
-            for c in range(2):
-                v = [q_s[p, k, m * PIECE + c * 12:m * PIECE + c * 12 + 12] for m in range(2)]
-                z = jnp.zeros((4, PART), f32)
-                u_s[p, k, c] = jnp.concatenate([v[0], z, v[1], z], axis=0).astype(bf16)
-        for rel in range(2):
-            for d in range(1 - rel, 4):
-                c = core if rel == 0 else 1 - core
-                cp = remote(u_s.at[p, lax.rem(pos[axis] + d, 4), c], l_r.at[p, rel, d], ss3.at[p, rel, d],
-                            rs3.at[p, rel, d], device(away(pos, axis, d), c))
-                cp.start()
-                last[p, rel, d] = cp
+        finish_part(1, p)
+    take(0)
     for i, c in enumerate(edge2):
         c.wait_recv()
         tot = tot + e2_r[i]
-    e_out[...] = pltpu.roll(tot * FACTOR, lax.rem(128 - 12 * head, 128), 1)
-    for p in range(3):
-        for rel in range(2):
-            v = u_s[p, pos[ORDER[p][2]], core].astype(f32) if rel == 0 else None
-            for d in range(1 - rel, 4):
-                last[p, rel, d].wait_recv()
-                t = l_r[p, rel, d].astype(f32)
-                v = t if v is None else v + t
-            g_out[:, columns((mine if rel == 0 else theirs) + p)] = v * FACTOR
+    ee_s[...] = pltpu.roll(tot * FACTOR, lax.rem(128 - 12 * head, 128), 1)
+    out_copies[2].start()
+    take(1)
     for m in range(2):
         for p in range(3):
             rings1[m][p].drain()
             rings2[m][p].drain()
     for c in list(pair.values()) + edge1 + edge2 + list(last.values()):
         c.wait_send()
-    for c in stores:
+    for c in stores + out_copies:
         c.wait()
 
 
@@ -451,37 +488,45 @@
         kernel,
         out_shape=[O((ROWS, 3 * W), f32), O((32, W), f32), O((2 * C, 128), f32)],
         in_specs=[pl.BlockSpec(memory_space=pltpu.SMEM), hbm, v, v, v, v, hbm, hbm, v],
-        out_specs=[hbm, v, v],
+        out_specs=[hbm, hbm, hbm],
         scratch_shapes=[
             V((ROWS, 3 * W), bf16), V((C, R), bf16), V((R, W), f32), V((R, W), f32), V((R, 1), f32), V((R, W), f32),
-            V((R, W), f32), V((R, 1), f32), big, V((C, R), bf16), V((R, 8), f32), V((R, 128), f32), V((R, 128), f32),
+            V((R, W), f32), V((R, W), f32), V((R, 1), f32), big, V((C, R), bf16), V((R, 8), f32), V((R, 128), f32), V((R, 128), f32),
             two, two, big, half, big, half, V((ROWS, 3 * W), f32), V((W, W), bf16), V((W, W), bf16),
-            V((2, 3, 4, 2, 192, PART), bf16), V((2, 3, 6, 192, PART), bf16),
+            V((2, 384, HALF), f32), V((2, 3, 4, 2, 192, PART), bf16), V((2, 3, 6, 192, PART), bf16),
             V((2, 3, 4, 2, 48, PART), bf16), V((2, 3, 6, 48, PART), bf16),
-            V((3, 4, 48, PART), f32), V((3, 4, 2, 32, PART), bf16), V((3, 2, 4, 32, PART), bf16),
+            V((2, 3, 4, 2, 16, PART), bf16), V((2, 3, 2, 4, 16, PART), bf16),
             V((2 * C, W + 128), f32), V((SEQ, 2 * C, 128), bf16), V((SEQ - 1, 2 * C, 128), bf16),
-            V((2 * C, 128), f32), V((HEAD - 1, 2 * C, 128), f32),
-            D((3,)), D((3,)), D((8,)), D((8,)), D((2, 3, 6)), D((2, 3, 6)), D((2, 3, 6)), D((2, 3, 6)),
-            D((3, 2, 4)), D((3, 2, 4)), D((SEQ - 1,)), D((SEQ - 1,)), D((HEAD - 1,)), D((HEAD - 1,)),
+            V((2 * C, 128), f32), V((HEAD - 1, 2 * C, 128), f32), V((32, W), f32), V((2 * C, 128), f32),
+            D((3, 4)), D((3,)), D((4,)), D((4,)), D((2, 3, 6)), D((2, 3, 6)), D((2, 3, 6)), D((2, 3, 6)),
+            D((2, 3, 2, 4)), D((2, 3, 2, 4)), D((SEQ - 1,)), D((SEQ - 1,)), D((HEAD - 1,)), D((HEAD - 1,)), D((3,)),
         ],
         compiler_params=pltpu.CompilerParams(
-            collective_id=0, has_side_effects=True, vmem_limit_bytes=60 * 1024 * 1024),
+            collective_id=0, has_side_effects=True, vmem_limit_bytes=62 * 1024 * 1024),
         cost_estimate=pl.CostEstimate(flops=12 * R * W * W, bytes_accessed=20_000_000, transcendentals=R * W),
     )(cnt, mod, lat.T, noise.T, times.T, inw, fc1, fc2, outw)
 
 
-def split_kernel(mod_hbm, g, e, mod_out, fc1_out, fc2_out, in_out, out_out, buf, in_sem, out_sem):
+def split_kernel(mod_hbm, g_hbm, e_hbm, mod_out, fc1_out, fc2_out, in_out, out_out,
+                 buf, g, e, fc1_s, fc2_s, in_s, out_s, in_sem, out_sem):
     n = ROWS // SPLIT
     parts = [pl.ds(i * n, n) for i in range(SPLIT)]
-    into = [pltpu.make_async_copy(mod_hbm.at[r], buf.at[r], in_sem.at[i]) for i, r in enumerate(parts)]
-    out = [pltpu.make_async_copy(buf.at[r], mod_out.at[r], out_sem.at[i]) for i, r in enumerate(parts)]
+    into = [pltpu.make_async_copy(src, dst, in_sem.at[SPLIT + i]) for i, (src, dst) in enumerate(((g_hbm, g), (e_hbm, e)))]
+    into += [pltpu.make_async_copy(mod_hbm.at[r], buf.at[r], in_sem.at[i]) for i, r in enumerate(parts)]
+    small = ((fc1_s, fc1_out), (fc2_s, fc2_out), (in_s, in_out), (out_s, out_out))
+    out = [pltpu.make_async_copy(src, dst, out_sem.at[SPLIT + i]) for i, (src, dst) in enumerate(small)]
+    out += [pltpu.make_async_copy(buf.at[r], mod_out.at[r], out_sem.at[i]) for i, r in enumerate(parts)]
     for c in into:
         c.start()
-    fc2_out[...] = g[0:12]
-    fc1_out[...] = g[16:28]
-    in_out[...] = e[0:C, 0:12]
-    out_out[...] = e[C:2 * C, 0:12]
-    for a, b in zip(into, out):
+    into[0].wait()
+    into[1].wait()
+    fc2_s[...] = g[0:12]
+    fc1_s[...] = g[16:28]
+    in_s[...] = e[0:C, 0:12]
+    out_s[...] = e[C:2 * C, 0:12]
+    for c in out[:4]:
+        c.start()
+    for a, b in zip(into[2:], out[4:]):
         a.wait()
         b.start()
     for c in out:
@@ -489,15 +534,17 @@
 
 
 def split_call(mod_grad, g, e):
-    v = pl.BlockSpec(memory_space=pltpu.VMEM)
     hbm = pl.BlockSpec(memory_space=pl.ANY)
     O = jax.ShapeDtypeStruct
+    V = pltpu.VMEM
     return pl.pallas_call(
         split_kernel,
         out_shape=[O((ROWS, 3 * W), f32), O((12, W), f32), O((12, W), f32), O((C, 12), f32), O((C, 12), f32)],
-        in_specs=[hbm, v, v],
-        out_specs=[hbm, v, v, v, v],
-        scratch_shapes=[pltpu.VMEM((ROWS, 3 * W), f32), pltpu.SemaphoreType.DMA((SPLIT,)), pltpu.SemaphoreType.DMA((SPLIT,))],
+        in_specs=[hbm] * 3,
+        out_specs=[hbm] * 5,
+        scratch_shapes=[V((ROWS, 3 * W), f32), V((32, W), f32), V((2 * C, 128), f32), V((12, W), f32), V((12, W), f32),
+                        V((C, 12), f32), V((C, 12), f32),
+                        pltpu.SemaphoreType.DMA((SPLIT + 2,)), pltpu.SemaphoreType.DMA((SPLIT + 4,))],
         compiler_params=pltpu.CompilerParams(vmem_limit_bytes=60 * 1024 * 1024),
     )(mod_grad, g, e)
 

time: 61.4 us -> 56.1 us (0.914)
  Pallas kernels: 59.7 us -> 54.4 us
    pallas_call x1, Pallas kernels: 55.6 us -> 51.7 us  [fused_call(): pl.pallas_call(kernel, out_shape=[O((ROWS, 3 * W), f32), O((32, W), f32),...]
    pallas_call x1, Pallas kernels: 4.14 us -> 2.71 us  [split_call(): pl.pallas_call(split_kernel, out_shape=[O((ROWS, 3 * W), f32), O((12, W),...]
where the time goes in v4:
time: 56.1 us; the launch traced here: 55.9 us
  Pallas kernels  54.4 us (97%)
  between operations  1.45 us (3%)
    pallas_call x1, Pallas kernels, fused_call(): pl.pallas_call(kernel, out_shape=[O((ROWS, 3 * W), f32), O((32, W), f32),...  51.7 us
    pallas_call x1, Pallas kernels, split_call(): pl.pallas_call(split_kernel, out_shape=[O((ROWS, 3 * W), f32), O((12, W),...  2.71 us

profile of v4, /device:TPU:1, one launch (start us, length us, event | category | flops | bytes accessed | tf_op | source)
XLA Modules:
  0.0 55.9 jit_solution(15943190264379692535)
XLA Ops:
  1.3 51.7 %shard_map.128 = (f32[128,4608]{1,0:T(8,128)}, f32[32,1536]{1,0:T(8,128)}, f32[32,128]{1,0:T(8,128)}) custom-call(s32[1]{0:T(128)S(6)} %copy.14.cnt, bf16[128,4608]{1,0:T(8,128)(2,1)} %mod_in.1, bf16[16,128]{1,0:T(8,128)(2,1)} %bitcast.4, bf16[64,128]{1,0:T(8,128)(2,1)} %bitcast.3, bf16[4,128]{1,0:T(4,128)(2,1)} %bitcast.5, bf16[16,1536]{1,0:T(8,128)(2,1)} %inw.1, ...), custom_call_target="tpu_custom_call" | custom-call | flops 14495514624 | bytes 20000000 | tf_op jit(solution)/shard_map/pallas_call | solution.py:487
  53.0 2.7 %shard_map.129 = (f32[128,4608]{1,0:T(8,128)}, f32[12,1536]{1,0:T(8,128)}, f32[12,1536]{1,0:T(8,128)}, f32[16,12]{1,0:T(8,128)}, f32[16,12]{1,0:T(8,128)}) custom-call(f32[128,4608]{1,0:T(8,128)} %get-tuple-element.8.mod_hbm, f32[32,1536]{1,0:T(8,128)} %get-tuple-element.9.g_hbm, f32[32,128]{1,0:T(8,128)} %get-tuple-element.10.e_hbm), custom_call_target="tpu_custom_call" | custom-call | tf_op jit(solution)/shard_map/pallas_call | solution.py:540

commit v5 on v4

--- a/solution.py
+++ b/solution.py
@@ -296,9 +296,9 @@
         prev = g2
 
 
-def kernel(cnt, mod_in, lat, noise, times, inw, fc1_hbm, fc2_hbm, outw,
+def kernel(cnt, mod_in, lat_hbm, noise_hbm, times_hbm, inw_hbm, fc1_hbm, fc2_hbm, outw_hbm,
            mod_hbm, g_out, e_out,
-           mod, noisy_s, st_s, ni_s, ri_s, d_s, bo_s, sg_s, ro_s, fin_s, pd_s, m_s, a1_s, a2_s,
+           mod, lat, noise, times, inw, outw, noisy_s, st_s, ni_s, ri_s, d_s, bo_s, sg_s, ro_s, fin_s, pd_s, m_s, a1_s, a2_s,
            hx, bix, bg, bgx, pg, pgx, mod_out, fc1, fc2,
            acc, s1, r1, s2, r2, u_s, l_r, e_s, ec_s, ec_r, e2_s, e2_r, g_s, ee_s,
            load_sem, store_sem, pair_ss, pair_rs, ss1, rs1, ss2, rs2, ss3, rs3, ess, ers, fss, frs, out_sem):
@@ -313,15 +313,17 @@
         for c in copies:
             c.wait()
 
+    small = [pltpu.make_async_copy(src, dst, load_sem.at[2, i + 1]) for i, (src, dst) in enumerate(
+        ((lat_hbm, lat), (noise_hbm, noise), (inw_hbm, inw), (outw_hbm, outw), (times_hbm, times)))]
     mod_load = pltpu.make_async_copy(mod_in, mod, load_sem.at[2, 0])
-    mod_load.start()
     fc1_load, fc2_load = load(0, fc1_hbm, fc1), load(1, fc2_hbm, fc2)
-    for c in fc1_load:
+    for c in small + [mod_load] + fc1_load:
         c.start()
     met = peers(pos, core)
     for dev in met:
         pl.semaphore_signal(barrier, inc=1, device_id=dev, device_id_type=MESH)
 
+    wait(small)
     make_noisy(lat, noise, times, noisy_s)
     stream(noisy_s, inw, st_s)
     mod_load.wait()
@@ -370,7 +372,7 @@
         pass3(m, p)
         axis = ORDER[p][2]
         for rel in range(2):
-            for d in range(1 - rel, 4):
+            for d in (2, 1, 3, 0)[:3 + rel]:
                 c = core if rel == 0 else 1 - core
                 cp = remote(u_s.at[m, p, lax.rem(pos[axis] + d, 4), c], l_r.at[m, p, rel, d], ss3.at[m, p, rel, d],
                             rs3.at[m, p, rel, d], device(away(pos, axis, d), c))
@@ -487,10 +489,10 @@
     return pl.pallas_call(
         kernel,
         out_shape=[O((ROWS, 3 * W), f32), O((32, W), f32), O((2 * C, 128), f32)],
-        in_specs=[pl.BlockSpec(memory_space=pltpu.SMEM), hbm, v, v, v, v, hbm, hbm, v],
+        in_specs=[pl.BlockSpec(memory_space=pltpu.SMEM), hbm, hbm, hbm, hbm, hbm, hbm, hbm, hbm],
         out_specs=[hbm, hbm, hbm],
         scratch_shapes=[
-            V((ROWS, 3 * W), bf16), V((C, R), bf16), V((R, W), f32), V((R, W), f32), V((R, 1), f32), V((R, W), f32),
+            V((ROWS, 3 * W), bf16), V((C, ROWS), bf16), V((DRAWS * C, ROWS), bf16), V((DRAWS, ROWS), bf16), V((C, W), bf16), V((C, W), bf16), V((C, R), bf16), V((R, W), f32), V((R, W), f32), V((R, 1), f32), V((R, W), f32),
             V((R, W), f32), V((R, W), f32), V((R, 1), f32), big, V((C, R), bf16), V((R, 8), f32), V((R, 128), f32), V((R, 128), f32),
             two, two, big, half, big, half, V((ROWS, 3 * W), f32), V((W, W), bf16), V((W, W), bf16),
             V((2, 384, HALF), f32), V((2, 3, 4, 2, 192, PART), bf16), V((2, 3, 6, 192, PART), bf16),
@@ -498,7 +500,7 @@
             V((2, 3, 4, 2, 16, PART), bf16), V((2, 3, 2, 4, 16, PART), bf16),
             V((2 * C, W + 128), f32), V((SEQ, 2 * C, 128), bf16), V((SEQ - 1, 2 * C, 128), bf16),
             V((2 * C, 128), f32), V((HEAD - 1, 2 * C, 128), f32), V((32, W), f32), V((2 * C, 128), f32),
-            D((3, 4)), D((3,)), D((4,)), D((4,)), D((2, 3, 6)), D((2, 3, 6)), D((2, 3, 6)), D((2, 3, 6)),
+            D((3, 6)), D((3,)), D((4,)), D((4,)), D((2, 3, 6)), D((2, 3, 6)), D((2, 3, 6)), D((2, 3, 6)),
             D((2, 3, 2, 4)), D((2, 3, 2, 4)), D((SEQ - 1,)), D((SEQ - 1,)), D((HEAD - 1,)), D((HEAD - 1,)), D((3,)),
         ],
         compiler_params=pltpu.CompilerParams(

time: 56.1 us -> 55.2 us (0.984)
  Pallas kernels: 54.4 us -> 53.6 us
    pallas_call x1, Pallas kernels: 51.7 us -> 50.9 us  [fused_call(): pl.pallas_call(kernel, out_shape=[O((ROWS, 3 * W), f32), O((32, W), f32),...]
where the time goes in v5:
time: 55.2 us; the launch traced here: 55.1 us
  Pallas kernels  53.6 us (97%)
  between operations  1.45 us (3%)
    pallas_call x1, Pallas kernels, fused_call(): pl.pallas_call(kernel, out_shape=[O((ROWS, 3 * W), f32), O((32, W), f32),...  50.9 us
    pallas_call x1, Pallas kernels, split_call(): pl.pallas_call(split_kernel, out_shape=[O((ROWS, 3 * W), f32), O((12, W),...  2.71 us

profile of v5, /device:TPU:1, one launch (start us, length us, event | category | flops | bytes accessed | tf_op | source)
XLA Modules:
  0.0 55.1 jit_solution(8403575609958409543)
XLA Ops:
  1.3 50.9 %shard_map.128 = (f32[128,4608]{1,0:T(8,128)}, f32[32,1536]{1,0:T(8,128)}, f32[32,128]{1,0:T(8,128)}) custom-call(s32[1]{0:T(128)S(6)} %copy.14.cnt, bf16[128,4608]{1,0:T(8,128)(2,1)} %mod_in.1, bf16[16,128]{1,0:T(8,128)(2,1)} %bitcast.4, bf16[64,128]{1,0:T(8,128)(2,1)} %bitcast.3, bf16[4,128]{1,0:T(4,128)(2,1)} %bitcast.5, bf16[16,1536]{1,0:T(8,128)(2,1)} %inw_hbm.1, ...), custom_call_target="tpu_custom_call" | custom-call | flops 14495514624 | bytes 20000000 | tf_op jit(solution)/shard_map/pallas_call | solution.py:489
  52.2 2.7 %shard_map.129 = (f32[128,4608]{1,0:T(8,128)}, f32[12,1536]{1,0:T(8,128)}, f32[12,1536]{1,0:T(8,128)}, f32[16,12]{1,0:T(8,128)}, f32[16,12]{1,0:T(8,128)}) custom-call(f32[128,4608]{1,0:T(8,128)} %get-tuple-element.8.mod_hbm, f32[32,1536]{1,0:T(8,128)} %get-tuple-element.9.g_hbm, f32[32,128]{1,0:T(8,128)} %get-tuple-element.10.e_hbm), custom_call_target="tpu_custom_call" | custom-call | tf_op jit(solution)/shard_map/pallas_call | solution.py:542

commit v6 on v5

--- a/solution.py
+++ b/solution.py
@@ -447,8 +447,6 @@
     for p in range(3):
         pass2(1, p)
     last = {}
-    for p in range(3):
-        finish_part(0, p)
     tot = ec_s[seq].astype(f32)
     for i, c in enumerate(edge1):
         c.wait_recv()
@@ -458,6 +456,8 @@
              for d in range(1, HEAD)]
     for c in edge2:
         c.start()
+    for p in range(3):
+        finish_part(0, p)
     for p in range(3):
         finish_part(1, p)
     take(0)

time: 55.2 us -> 55.3 us (level)
  no operation moved by 1% of the time
where the time goes in v6:
time: 55.3 us; the launch traced here: 55.1 us
  Pallas kernels  53.7 us (97%)
  between operations  1.45 us (3%)
    pallas_call x1, Pallas kernels, fused_call(): pl.pallas_call(kernel, out_shape=[O((ROWS, 3 * W), f32), O((32, W), f32),...  50.9 us
    pallas_call x1, Pallas kernels, split_call(): pl.pallas_call(split_kernel, out_shape=[O((ROWS, 3 * W), f32), O((12, W),...  2.71 us

profile of v6, /device:TPU:1, one launch (start us, length us, event | category | flops | bytes accessed | tf_op | source)
XLA Modules:
  0.0 55.1 jit_solution(10754002190945356734)
XLA Ops:
  1.3 50.9 %shard_map.128 = (f32[128,4608]{1,0:T(8,128)}, f32[32,1536]{1,0:T(8,128)}, f32[32,128]{1,0:T(8,128)}) custom-call(s32[1]{0:T(128)S(6)} %copy.14.cnt, bf16[128,4608]{1,0:T(8,128)(2,1)} %mod_in.1, bf16[16,128]{1,0:T(8,128)(2,1)} %bitcast.4, bf16[64,128]{1,0:T(8,128)(2,1)} %bitcast.3, bf16[4,128]{1,0:T(4,128)(2,1)} %bitcast.5, bf16[16,1536]{1,0:T(8,128)(2,1)} %inw_hbm.1, ...), custom_call_target="tpu_custom_call" | custom-call | flops 14495514624 | bytes 20000000 | tf_op jit(solution)/shard_map/pallas_call | solution.py:489
  52.2 2.7 %shard_map.129 = (f32[128,4608]{1,0:T(8,128)}, f32[12,1536]{1,0:T(8,128)}, f32[12,1536]{1,0:T(8,128)}, f32[16,12]{1,0:T(8,128)}, f32[16,12]{1,0:T(8,128)}) custom-call(f32[128,4608]{1,0:T(8,128)} %get-tuple-element.8.mod_hbm, f32[32,1536]{1,0:T(8,128)} %get-tuple-element.9.g_hbm, f32[32,128]{1,0:T(8,128)} %get-tuple-element.10.e_hbm), custom_call_target="tpu_custom_call" | custom-call | tf_op jit(solution)/shard_map/pallas_call | solution.py:542
